TPU v7x, 128 devices: a whole 4x4x4 slice. The times are simulated.
128 devices in a mesh: row: 16 (over y, x), col: 8 (over z, core).
Axes of the slice: x: 4, y: 4, z: 4, core: 2. Of those that a mesh axis runs over, the one named last changes fastest.
Arguments:
- emission: float32 [16, 1048576], P(None, ('row', 'col')), may hold values from -6 to 6
- basis_source: bfloat16 [64, 1048576], P(None, ('row', 'col')), may hold values from -0.5 to 0.5
- basis_target: bfloat16 [64, 1048576], P(None, ('row', 'col')), may hold values from -0.75 to 0.75
- local_transfer: bfloat16 [16128, 64, 64], P(('row', 'col')), may hold values from -0.5 to 0.5
- local_sibling: bfloat16 [7936, 64, 64], P(('row', 'col')), as said below
- upper_transfer: bfloat16 [254, 64, 64], replicated, may hold values from -0.5 to 0.5
- upper_sibling: bfloat16 [254, 64, 64], replicated, as said below
- leaf_source: int32 [8192, 4], P(('row', 'col')), may hold values from 0 to 8191, as said below
- leaf_coupling: bfloat16 [8192, 4, 64, 64], P(('row', 'col')), may hold values from -0.375 to 0.375
- near_block: bfloat16 [24576, 128, 128], P(('row', 'col')), may hold values from -0.5 to 0.5
- near_target: int32 [24576], P(('row', 'col')), may hold values from 0 to 8191, as said below
- near_source: int32 [24576], P(('row', 'col')), may hold values from 0 to 8191, as said below
- near_count: int32 [128], P(('row', 'col')), may hold values from 66 to 192, as said below
Outputs:
- irradiance: float32 [16, 1048576], P(None, ('row', 'col'))
Inputs may be any that keep to these rules, and one draw needn't show every extreme that they name: leaf_source[t, j] lies in the row subtree of t (the same block of 512 leaves) and differs from t by 2 or more. `near_target`: the slots of device d name target leaves of device d only; the first 64 slots of each device hold every leaf of the device once, as its own source. `near_source`: each slot's source leaf lies within one leaf of its target leaf. `near_count`: some device uses all of its slots. `local_sibling`: coupling matrices of clusters higher in the tree are larger in magnitude. `upper_sibling`: coupling matrices of clusters higher in the tree are larger in magnitude.
All inputs are finite; a program needn't handle non-finite values.
Results may differ from a plain program's by a relative error of at most 0.0005.
Values sent between devices are 32-bit elements; how exact they have to be, the bound alone decides.
A program may use at most 128 MiB of HBM per device.

v0:
```python
import jax
import jax.numpy as jnp
from jax import lax
from jax.sharding import PartitionSpec as P

RANK = 64
RHS = 16


highest = lax.Precision.HIGHEST


def swapped_2(value, axis, apart):
    mask = 2**apart
    pairs = [(source, source ^ mask) for source in range(lax.axis_size(axis))]
    return lax.ppermute(value, axis, pairs)


def with_halo(cells, sides, width):
    for axis, dim in sides:
        count = lax.axis_size(axis)
        ends = count - 1
        head = lax.slice_in_dim(cells, 0, width, axis=dim)
        tail = lax.slice_in_dim(cells, cells.shape[dim] - width, cells.shape[dim], axis=dim)
        cells = jnp.concatenate(
            [
                lax.ppermute(tail, axis, [(i, (i + 1) % count) for i in range(ends)]),
                cells,
                lax.ppermute(head, axis, [((i + 1) % count, i) for i in range(ends)]),
            ],
            axis=dim,
        )
    return cells


def upward(transfer, coefficients):
    lifted = jnp.einsum(
        "cba,cbr->car", transfer.astype(jnp.float32), coefficients, precision=highest
    )
    paired = lifted.reshape(lifted.shape[0] // 2, 2, RANK, RHS)
    return paired[:, 0] + paired[:, 1]


def downward(transfer, parents):
    spread = jnp.repeat(parents, 2, axis=0)
    return jnp.einsum("cab,cbr->car", transfer.astype(jnp.float32), spread, precision=highest)


def swapped(coefficients):
    cluster_count = coefficients.shape[0]
    return coefficients.reshape(cluster_count // 2, 2, RANK, RHS)[:, ::-1].reshape(
        cluster_count, RANK, RHS
    )


def couple(coupling, coefficients):
    return jnp.einsum("cab,cbr->car", coupling.astype(jnp.float32), coefficients, precision=highest)


def pick_row(matrices, position):
    return lax.dynamic_index_in_dim(matrices, position, 0, keepdims=False).astype(jnp.float32)


def shards(
    emission,
    basis_source,
    basis_target,
    local_transfer,
    local_sibling,
    upper_transfer,
    upper_sibling,
    leaf_source,
    leaf_coupling,
    near_block,
    near_target,
    near_source,
    near_count,
):
    leaf_dev = leaf_source.shape[0]
    patch_count = emission.shape[1]
    leaf_size = patch_count // leaf_dev
    devices = lax.axis_size(("row", "col"))
    col_count = lax.axis_size("col")
    device = lax.axis_index(("row", "col"))
    height_local = leaf_dev.bit_length() - 1
    height_upper = devices.bit_length() - 1
    leaf_major = emission.reshape(RHS, leaf_dev, leaf_size).transpose(1, 0, 2)
    source_major = (
        basis_source.reshape(RANK, leaf_dev, leaf_size).transpose(1, 0, 2).astype(jnp.float32)
    )
    leaf_coef = jnp.einsum("lki,lri->lkr", source_major, leaf_major, precision=highest)
    group_first = lax.axis_index("row") * (leaf_dev * col_count)
    wanted = leaf_source - group_first
    flat_coef = leaf_coef.reshape(leaf_dev, RANK * RHS)
    portion = lax.all_gather(flat_coef, "col", axis=0, tiled=True)
    inside = (wanted >= 0) & (wanted < portion.shape[0])
    picked = jnp.take(portion, jnp.clip(wanted, 0, portion.shape[0] - 1), axis=0)
    partner_coef = jnp.where(inside[:, :, None], picked, 0.0)
    partner_coef = partner_coef.reshape(leaf_dev, leaf_source.shape[1], RANK, RHS)
    levels = [leaf_coef]
    for height in range(height_local):
        cluster_count = leaf_dev >> height
        offset = 2 * leaf_dev - 2 * cluster_count
        levels.append(upward(local_transfer[offset : offset + cluster_count], levels[-1]))
    root_coef = levels[-1]
    current = root_coef[0]
    partners = []
    own_rows = []
    for section_index in range(height_upper):
        partner = swapped_2(current, ("row", "col"), section_index)
        offset = 2 * devices - 2 * (devices >> section_index)
        cluster = jnp.right_shift(device, section_index)
        own_index = offset + cluster
        sibling_index = offset + jnp.bitwise_xor(cluster, 1)
        own_lift = jnp.dot(pick_row(upper_transfer, own_index).T, current, precision=highest)
        partner_lift = jnp.dot(
            pick_row(upper_transfer, sibling_index).T, partner, precision=highest
        )
        partners.append(partner)
        own_rows.append(own_index)
        current = own_lift + partner_lift
    far_root = jnp.zeros((RANK, RHS), jnp.float32)
    for section_index in range(height_upper - 1, -1, -1):
        coupled = jnp.dot(
            pick_row(upper_sibling, own_rows[section_index]),
            partners[section_index],
            precision=highest,
        )
        carried = jnp.dot(
            pick_row(upper_transfer, own_rows[section_index]), far_root, precision=highest
        )
        far_root = coupled + carried
    far_coef = far_root[None]
    for height in range(height_local - 1, -1, -1):
        cluster_count = leaf_dev >> height
        offset = 2 * leaf_dev - 2 * cluster_count
        carried = downward(local_transfer[offset : offset + cluster_count], far_coef)
        if height >= 1:
            first = leaf_dev - 2 * cluster_count
            far_coef = (
                couple(local_sibling[first : first + cluster_count], swapped(levels[height]))
                + carried
            )
        else:
            listed = jnp.einsum(
                "tjab,tjbr->tar", leaf_coupling.astype(jnp.float32), partner_coef, precision=highest
            )
            far_coef = listed + carried
    target_major = (
        basis_target.reshape(RANK, leaf_dev, leaf_size).transpose(1, 0, 2).astype(jnp.float32)
    )
    far_field = jnp.einsum("lkr,lki->lri", far_coef, target_major, precision=highest)
    extended = with_halo(leaf_major, ((("row", "col"), 0),), 1)
    group_size = near_block.shape[0] // 12
    live_count = near_count[0]
    rounds = (live_count + group_size - 1) // group_size
    leaf_first = device * leaf_dev
    leaf_ids = jnp.arange(leaf_dev, dtype=jnp.int32)
    slot_ids = jnp.arange(group_size, dtype=jnp.int32)

    def near_step(round_index, accumulated):
        offset = round_index * group_size
        blocks = lax.dynamic_slice_in_dim(near_block, offset, group_size, 0).astype(jnp.float32)
        target_local = lax.dynamic_slice_in_dim(near_target, offset, group_size, 0) - leaf_first
        source_local = lax.dynamic_slice_in_dim(near_source, offset, group_size, 0) - leaf_first + 1
        live_slot = offset + slot_ids < live_count
        picked = jnp.take(extended, source_local, axis=0)
        product = jnp.einsum("grj,gij->gri", picked, blocks, precision=highest)
        one_hot = ((target_local[:, None] == leaf_ids[None, :]) & live_slot[:, None]).astype(
            jnp.float32
        )
        return accumulated + jnp.einsum("gt,gri->tri", one_hot, product, precision=highest)

    near_field = lax.fori_loop(
        0, rounds, near_step, jnp.zeros((leaf_dev, RHS, leaf_size), jnp.float32)
    )
    total = far_field + near_field
    return total.transpose(1, 0, 2).reshape(RHS, patch_count)


def solution(mesh):
    in_specs = (
        P(None, ("row", "col")),
        P(None, ("row", "col")),
        P(None, ("row", "col")),
        P(("row", "col"), None, None),
        P(("row", "col"), None, None),
        P(),
        P(),
        P(("row", "col"), None),
        P(("row", "col"), None, None, None),
        P(("row", "col"), None, None),
        P(("row", "col")),
        P(("row", "col")),
        P(("row", "col")),
    )
    out_specs = P(None, ("row", "col"))
    return jax.shard_map(shards, mesh=mesh, in_specs=in_specs, out_specs=out_specs, check_vma=False)
```

profile of v0, /device:TPU:88, one launch (start us, length us, event | category | flops | bytes accessed | tf_op | source)
XLA Modules:
  0.0 250.5 jit_solution(11210937205281134059)
XLA Ops:
  6.5 2.7 %slice.85 = bf16[32,64,64]{0,2,1:T(8,128)(2,1)} slice(bf16[126,64,64]{0,2,1:T(8,128)(2,1)} %param.18), slice={[64:96], [0:64], [0:64]} | slice | bytes 524288 | tf_op jit(solution)/shard_map/slice | solution.py:137
  9.3 2.6 %slice.89 = bf16[16,64,64]{0,2,1:T(8,128)(2,1)} slice(bf16[126,64,64]{0,2,1:T(8,128)(2,1)} %param.18), slice={[96:112], [0:64], [0:64]} | slice | bytes 262144 | tf_op jit(solution)/shard_map/slice | solution.py:137
  17.0 1.6 copy.135
  18.7 3.5 %fusion.35 = f32[64,64,16]{1,2,0:T(8,128)S(1)} fusion(f32[64,16,128]{2,0,1:T(8,128)} %bitcast.266, bf16[64,8192]{1,0:T(8,128)(2,1)} %param.16), kind=kOutput, calls=%fused_computation.62 | convolution fusion | flops 100663296 | bytes 1835008 | tf_op jit(solution)/shard_map/lki,lri->lkr/dot_general | solution.py:91
  23.1 2.2 copy.138
  26.2 1.9 copy.141
  29.1 1.6 copy.144
  32.4 2.4 copy.147
  35.8 2.3 copy.151
  39.6 2.2 copy.89
  41.8 1.9 copy.90
  43.7 1.5 fusion.107
  45.2 2.4 collective-permute-start.7
  47.6 3.3 %collective-permute-start.8 = (f32[1,16,128]{2,0,1:T(1,128)}, f32[1,16,128]{2,0,1:T(1,128)}, u32[]{:S(2)}, u32[]{:S(2)}) collective-permute-start(f32[1,16,128]{2,0,1:T(1,128)} %get-tuple-element.230), channel_id=1, source_target_pairs={{1,0},{2,1},{3,2},{4,3},{5,4},{6,5},{7,6},{8,7},{9,8},{10,9},{11,1... | collective-permute-start | bytes 24584 | tf_op jit(solution)/shard_map/ppermute | solution.py:29
  51.6 7.3 %constant_dynamic-slice_fusion.1 = (bf16[1,64,64]{0,2,1:T(8,128)(2,1)}, bf16[1,64,64]{0,2,1:T(8,128)(2,1)}, bf16[1,64,64]{0,2,1:T(8,128)(2,1)}, bf16[1,64,64]{0,...) fusion(bf16[254,64,64]{0,2,1:T(8,128)(2,1)S(1)} %copy-done.1, ...), kind=kLoop, calls=%fused_computation.146 | loop fusion | bytes 213044 | tf_op jit(solution)/shard_map/jit(dynamic_index_in_dim)/dynamic_slice | solution.py:61
  58.9 1.8 copy.152
  62.1 2.3 copy.170
  65.9 5.2 %constant_dynamic-slice_fusion.19 = (bf16[1,64,64]{0,2,1:T(8,128)(2,1)}, bf16[1,64,64]{0,2,1:T(8,128)(2,1)}, bf16[1,64,64]{0,2,1:T(8,128)(2,1)}, bf16[1,64,64]{0...) fusion(bf16[254,64,64]{0,2,1:T(8,128)(2,1)S(1)} %copy-done.3, ...), kind=kLoop, calls=%fused_computation.164 | loop fusion | bytes 114716 | tf_op jit(solution)/shard_map/jit(dynamic_index_in_dim)/dynamic_slice | solution.py:61
  71.8 1.5 fusion.58
  73.3 1.7 fusion.53
  75.8 1.9 fusion.48
  78.6 2.1 fusion.43
  81.7 2.8 %fusion.38 = f32[32,16,64]{2,1,0:T(8,128)} fusion(f32[32,64,16]{1,2,0:T(8,128)S(1)} %bitcast.275, bf16[62,64,64]{2,1,0:T(8,128)(2,1)} %param.19), kind=kOutput, calls=%fused_computation.67 | convolution fusion | flops 25165824 | bytes 786432 | tf_op jit(solution)/shard_map/cab,cbr->car/dot_general | solution.py:57
  86.1 2.4 copy.154
  88.4 2.3 copy.155
  90.7 2.3 copy.157
  93.0 2.3 copy.158
  95.2 2.3 copy.160
  97.5 2.3 copy.161
  99.8 2.3 copy.163
  103.6 1.8 copy.167
  105.4 1.7 copy.169
  107.1 2.3 copy.168
  109.4 2.3 copy.165
  111.7 2.3 copy.162
  114.0 2.3 copy.159
  116.3 2.3 copy.156
  118.6 2.3 copy.153
  124.1 1.6 collective-permute-start.1
  125.9 1.9 collective-permute-done.1
  127.9 4.6 %collective-permute-start.2 = (f32[64,16]{0,1:T(8,128)S(1)}, f32[64,16]{0,1:T(8,128)S(1)}, u32[]{:S(2)}, u32[]{:S(2)}) collective-permute-start(f32[64,16]{0,1:T(8,128)S(1)} %convolution_add_fusion.17), channel_id=1, source_target_pairs={{0,4},{1,5},{2,6},{3,7},{4,0},{5,1},{6,2},{7,3},{8,12},{9,13},{10,... | collective-permute-start | bytes 12296 | tf_op jit(solution)/shard_map/ppermute | solution.py:16
  135.0 2.9 %collective-permute-done.3 = f32[64,16]{0,1:T(8,128)S(1)} collective-permute-done((f32[64,16]{0,1:T(8,128)S(1)}, f32[64,16]{0,1:T(8,128)S(1)}, u32[]{:S(2)}, u32[]{:S(2)}) %collective-permute-start.3) | collective-permute-done | bytes 4128 | tf_op jit(solution)/shard_map/ppermute | solution.py:16
  138.1 2.2 collective-permute-start.4
  140.4 2.8 %collective-permute-done.4 = f32[64,16]{0,1:T(8,128)S(1)} collective-permute-done((f32[64,16]{0,1:T(8,128)S(1)}, f32[64,16]{0,1:T(8,128)S(1)}, u32[]{:S(2)}, u32[]{:S(2)}) %collective-permute-start.4) | collective-permute-done | bytes 4128 | tf_op jit(solution)/shard_map/ppermute | solution.py:16
  144.0 3.0 %collective-permute-done.5 = f32[64,16]{0,1:T(8,128)S(1)} collective-permute-done((f32[64,16]{0,1:T(8,128)S(1)}, f32[64,16]{0,1:T(8,128)S(1)}, u32[]{:S(2)}, u32[]{:S(2)}) %collective-permute-start.5) | collective-permute-done | bytes 4128 | tf_op jit(solution)/shard_map/ppermute | solution.py:16
  148.9 56.5 %while.13 = (s32[]{:T(128)}, f32[64,16,128]{2,0,1:T(8,128)S(1)}, s32[]{:T(128)}, s32[192]{0:T(256)S(1)}, s32[]{:T(128)}, /*index=5*/s32[]{:T(128)}, s32[192]{0:T...) while((s32[]{:T(128)}, f32[64,16,128]{2,0,1:T(8,128)S(1)}, ...), condition=%wide.region_1.2_spmd.clone, body=%wide.region_0.1_spmd.clone.sunk | while | flops 75664560 | bytes 2233031 | solution.py:174
  148.9 1.5 compare_and_fusion.4
  151.0 2.0 fusion.171
  155.7 2.0 fusion.171
  160.4 2.0 fusion.171
  165.1 2.0 fusion.171
  169.8 2.0 fusion.171
  174.5 2.0 fusion.171
  179.2 2.0 fusion.171
  183.9 2.0 fusion.171
  188.6 2.0 fusion.171
  193.3 2.0 fusion.171
  198.0 2.0 fusion.171
  202.7 2.0 fusion.171
  219.7 1.9 fusion.29
  221.5 3.2 %gather_fusion.1 = f32[256,1024]{1,0:T(8,128)S(1)} fusion(f32[512,1024]{1,0:T(8,128)} %all-gather.2.cloned.1.call-done, s32[1024]{0:T(1024)S(1)} %pad_clamp_fusion.1), kind=kCustom, calls=%fused_computation.1 | custom fusion | bytes 2098176 | tf_op jit(solution)/shard_map/jit(_take)/gather | solution.py:97
  224.7 4.9 %gather.14 = f32[64,4,64,16]{3,2,1,0:T(8,128)} reshape(f32[256,1024]{1,0:T(8,128)S(1)} %gather_fusion.1) | data formatting | bytes 2097152 | tf_op jit(solution)/shard_map/jit(_take)/gather | solution.py:97
  229.7 10.4 %fusion.26 = f32[64,16,64]{2,1,0:T(8,128)S(1)} fusion(bf16[64,4,64,64]{3,2,1,0:T(8,128)(2,1)} %param.23, f32[64,4,64,16]{3,2,1,0:T(8,128)} %gather.14, pred[64,4]{1,0:T(8,128)(4,1)S(1)} %copy-done.31, pred[64,4]{1,0:T(8,128)(4,1)S(1)} %copy-done.30), kind=kOutput, calls=%fused_computation.34 | convolution fusion | flops 201850880 | bytes 3408384 | tf_op jit(solution)/shard_map/tjab,tjbr->tar/dot_general | solution.py:145
  240.1 1.7 convolution_add_fusion.2
  (219 shorter events, 76.7 us)
Async XLA Ops:
  6.5 235.3 %copy-start = (bf16[64,8192]{1,0:T(8,128)(2,1)S(1)}, bf16[64,8192]{1,0:T(8,128)(2,1)}, u32[]{:S(2)}) copy-start(bf16[64,8192]{1,0:T(8,128)(2,1)} %param.17) | copy-start | bytes 3145732
  6.5 5.4 %copy-start.2 = (bf16[126,64,64]{0,2,1:T(8,128)(2,1)S(1)}, bf16[126,64,64]{0,2,1:T(8,128)(2,1)}, u32[]{:S(2)}) copy-start(bf16[126,64,64]{0,2,1:T(8,128)(2,1)} %param.18) | copy-start | bytes 3096580
  6.5 215.0 %all-gather.2.cloned.1.call-start = ((), (), s32[]{:S(2)}) async-start(), calls=%async_computation | async-start | bytes 2359296 | tf_op jit(solution)/shard_map/all_gather | solution.py:95
  9.3 6.8 %copy-start.16 = (f32[16,8192]{1,0:T(8,128)S(1)}, f32[16,8192]{1,0:T(8,128)}, u32[]{:S(2)}) copy-start(f32[16,8192]{1,0:T(8,128)} %param.15) | copy-start | bytes 1572868
  18.7 7.2 %copy-start.4 = (bf16[64,64,64]{2,1,0:T(8,128)(2,1)}, bf16[64,64,64]{2,1,0:T(8,128)(2,1)S(1)}, u32[]{:S(2)}) copy-start(bf16[64,64,64]{2,1,0:T(8,128)(2,1)S(1)} %copy.135) | copy-start | bytes 1572868
  22.1 0.9 copy-start.9
  23.1 2.7 %copy-start.13 = (f32[32,1,64,16]{2,3,0,1:T(8,128)}, f32[32,1,64,16]{2,3,0,1:T(8,128)S(1)}, u32[]{:S(2)}) copy-start(f32[32,1,64,16]{2,3,0,1:T(8,128)S(1)} %fusion.40) | copy-start | bytes 393220
  25.3 0.8 copy-start.7
  26.2 2.3 copy-start.14
  26.2 25.4 %copy-start.1 = (bf16[254,64,64]{0,2,1:T(8,128)(2,1)S(1)}, bf16[254,64,64]{0,2,1:T(8,128)(2,1)}, u32[]{:S(2)}) copy-start(bf16[254,64,64]{0,2,1:T(8,128)(2,1)} %param.20) | copy-start | bytes 6242308
  39.6 83.7 %collective-permute-start = (f32[64,16]{0,1:T(8,128)}, f32[64,16]{0,1:T(8,128)}, u32[]{:S(2)}, u32[]{:S(2)}) collective-permute-start(f32[64,16]{0,1:T(8,128)} %fusion.102), channel_id=1, source_target_pairs={{0,1},{1,0},{2,3},{3,2},{4,5},{5,4},{6,7},{7,6},{8,9},{9,8},{10,11... | collective-permute-start | bytes 12296 | tf_op jit(solution)/shard_map/ppermute | solution.py:16
  45.2 87.5 %collective-permute-start.7 = (f32[1,16,128]{2,0,1:T(1,128)}, f32[1,16,128]{2,0,1:T(1,128)}, u32[]{:S(2)}, u32[]{:S(2)}) collective-permute-start(f32[1,16,128]{2,0,1:T(1,128)} %get-tuple-element.229), channel_id=1, source_target_pairs={{0,1},{1,2},{2,3},{3,4},{4,5},{5,6},{6,7},{7,8},{8,9},{9,10},{10,1... | collective-permute-start | bytes 24584 | tf_op jit(solution)/shard_map/ppermute | solution.py:27
  47.6 85.1 %collective-permute-start.8 = (f32[1,16,128]{2,0,1:T(1,128)}, f32[1,16,128]{2,0,1:T(1,128)}, u32[]{:S(2)}, u32[]{:S(2)}) collective-permute-start(f32[1,16,128]{2,0,1:T(1,128)} %get-tuple-element.230), channel_id=1, source_target_pairs={{1,0},{2,1},{3,2},{4,3},{5,4},{6,5},{7,6},{8,7},{9,8},{10,9},{11,1... | collective-permute-start | bytes 24584 | tf_op jit(solution)/shard_map/ppermute | solution.py:29
  58.9 7.0 %copy-start.3 = (bf16[254,64,64]{0,2,1:T(8,128)(2,1)S(1)}, bf16[254,64,64]{0,2,1:T(8,128)(2,1)}, u32[]{:S(2)}) copy-start(bf16[254,64,64]{0,2,1:T(8,128)(2,1)} %param.21) | copy-start | bytes 6242308
  60.7 10.3 %copy-start.19 = (bf16[1,64,64]{2,1,0:T(8,128)(2,1)}, bf16[1,64,64]{2,1,0:T(8,128)(2,1)S(1)}, u32[]{:S(2)}) copy-start(bf16[1,64,64]{2,1,0:T(8,128)(2,1)S(1)} %copy.152) | copy-start | bytes 24580
  81.7 20.3 %copy-start.12 = (bf16[1,64,64]{0,2,1:T(8,128)(2,1)S(1)}, bf16[1,64,64]{0,2,1:T(8,128)(2,1)}, u32[]{:S(2)}) copy-start(bf16[1,64,64]{0,2,1:T(8,128)(2,1)} %get-tuple-element.219) | copy-start | bytes 24580
  86.1 17.1 %copy-start.11 = (bf16[1,64,64]{0,2,1:T(8,128)(2,1)S(1)}, bf16[1,64,64]{0,2,1:T(8,128)(2,1)}, u32[]{:S(2)}) copy-start(bf16[1,64,64]{0,2,1:T(8,128)(2,1)} %get-tuple-element.218) | copy-start | bytes 24580
  103.6 17.3 %copy-start.10 = (bf16[1,64,64]{0,2,1:T(8,128)(2,1)S(1)}, bf16[1,64,64]{0,2,1:T(8,128)(2,1)}, u32[]{:S(2)}) copy-start(bf16[1,64,64]{0,2,1:T(8,128)(2,1)} %get-tuple-element.209) | copy-start | bytes 24580
  105.4 38.5 %copy-start.25 = (bf16[1,64,64]{2,1,0:T(8,128)(2,1)}, bf16[1,64,64]{2,1,0:T(8,128)(2,1)S(1)}, u32[]{:S(2)}) copy-start(bf16[1,64,64]{2,1,0:T(8,128)(2,1)S(1)} %copy.167) | copy-start | bytes 24580
  105.4 18.0 %copy-start.29 = (bf16[1,64,64]{2,1,0:T(8,128)(2,1)S(1)}, bf16[1,64,64]{2,1,0:T(8,128)(2,1)}, u32[]{:S(2)}) copy-start(bf16[1,64,64]{2,1,0:T(8,128)(2,1)} %copy.154) | copy-start | bytes 24580
  105.4 18.0 %copy-start.37 = (f32[64,16]{0,1:T(8,128)S(1)}, f32[64,16]{0,1:T(8,128)}, u32[]{:S(2)}) copy-start(f32[64,16]{0,1:T(8,128)} %fusion.98) | copy-start | bytes 12292
  105.4 20.4 %copy-start.21 = (bf16[1,64,64]{2,1,0:T(8,128)(2,1)S(1)}, bf16[1,64,64]{2,1,0:T(8,128)(2,1)}, u32[]{:S(2)}) copy-start(bf16[1,64,64]{2,1,0:T(8,128)(2,1)} %copy.155) | copy-start | bytes 24580
  105.4 22.4 %copy-start.28 = (bf16[1,64,64]{2,1,0:T(8,128)(2,1)S(1)}, bf16[1,64,64]{2,1,0:T(8,128)(2,1)}, u32[]{:S(2)}) copy-start(bf16[1,64,64]{2,1,0:T(8,128)(2,1)} %copy.157) | copy-start | bytes 24580
  105.4 27.2 %copy-start.22 = (bf16[1,64,64]{2,1,0:T(8,128)(2,1)S(1)}, bf16[1,64,64]{2,1,0:T(8,128)(2,1)}, u32[]{:S(2)}) copy-start(bf16[1,64,64]{2,1,0:T(8,128)(2,1)} %copy.158) | copy-start | bytes 24580
  105.4 27.3 %copy-start.6 = (f32[2,8,64,128]{3,2,1,0:T(8,128)S(1)}, f32[2,8,64,128]{3,2,1,0:T(8,128)}, u32[]{:S(2)}) copy-start(f32[2,8,64,128]{3,2,1,0:T(8,128)} %copy.174) | copy-start | bytes 1572868
  109.4 24.8 %copy-start.27 = (bf16[1,64,64]{2,1,0:T(8,128)(2,1)S(1)}, bf16[1,64,64]{2,1,0:T(8,128)(2,1)}, u32[]{:S(2)}) copy-start(bf16[1,64,64]{2,1,0:T(8,128)(2,1)} %copy.160) | copy-start | bytes 24580
  109.4 25.5 %copy-start.23 = (bf16[1,64,64]{2,1,0:T(8,128)(2,1)S(1)}, bf16[1,64,64]{2,1,0:T(8,128)(2,1)}, u32[]{:S(2)}) copy-start(bf16[1,64,64]{2,1,0:T(8,128)(2,1)} %copy.161) | copy-start | bytes 24580
  111.7 26.3 %copy-start.26 = (bf16[1,64,64]{2,1,0:T(8,128)(2,1)S(1)}, bf16[1,64,64]{2,1,0:T(8,128)(2,1)}, u32[]{:S(2)}) copy-start(bf16[1,64,64]{2,1,0:T(8,128)(2,1)} %copy.163) | copy-start | bytes 24580
  111.7 28.6 %copy-start.24 = (bf16[1,64,64]{2,1,0:T(8,128)(2,1)S(1)}, bf16[1,64,64]{2,1,0:T(8,128)(2,1)}, u32[]{:S(2)}) copy-start(bf16[1,64,64]{2,1,0:T(8,128)(2,1)} %copy.164) | copy-start | bytes 24580
  111.7 37.1 %copy-start.38 = (s32[192]{0:T(256)S(1)}, s32[192]{0:T(256)}, u32[]{:S(2)}) copy-start(s32[192]{0:T(256)} %param.25) | copy-start | bytes 2308
  124.1 3.7 %collective-permute-start.1 = (f32[64,16]{0,1:T(8,128)S(1)}, f32[64,16]{0,1:T(8,128)S(1)}, u32[]{:S(2)}, u32[]{:S(2)}) collective-permute-start(f32[64,16]{0,1:T(8,128)S(1)} %convolution_add_fusion.19), channel_id=1, source_target_pairs={{0,2},{1,3},{2,0},{3,1},{4,6},{5,7},{6,4},{7,5},{8,10},{9,11},{10,... | collective-permute-start | bytes 12296 | tf_op jit(solution)/shard_map/ppermute | solution.py:16
  127.8 21.0 %copy-start.32 = (f32[64,16]{0,1:T(8,128)}, f32[64,16]{0,1:T(8,128)S(1)}, u32[]{:S(2)}) copy-start(f32[64,16]{0,1:T(8,128)S(1)} %collective-permute-done.1) | copy-start | bytes 12292
  127.9 6.3 %collective-permute-start.2 = (f32[64,16]{0,1:T(8,128)S(1)}, f32[64,16]{0,1:T(8,128)S(1)}, u32[]{:S(2)}, u32[]{:S(2)}) collective-permute-start(f32[64,16]{0,1:T(8,128)S(1)} %convolution_add_fusion.17), channel_id=1, source_target_pairs={{0,4},{1,5},{2,6},{3,7},{4,0},{5,1},{6,2},{7,3},{8,12},{9,13},{10,... | collective-permute-start | bytes 12296 | tf_op jit(solution)/shard_map/ppermute | solution.py:16
  134.2 14.6 %copy-start.33 = (f32[64,16]{0,1:T(8,128)}, f32[64,16]{0,1:T(8,128)S(1)}, u32[]{:S(2)}) copy-start(f32[64,16]{0,1:T(8,128)S(1)} %collective-permute-done.2) | copy-start | bytes 12292
  134.3 3.7 %collective-permute-start.3 = (f32[64,16]{0,1:T(8,128)S(1)}, f32[64,16]{0,1:T(8,128)S(1)}, u32[]{:S(2)}, u32[]{:S(2)}) collective-permute-start(f32[64,16]{0,1:T(8,128)S(1)} %convolution_add_fusion.15), channel_id=1, source_target_pairs={{0,8},{1,9},{2,10},{3,11},{4,12},{5,13},{6,14},{7,15},{8,0},{9,1},... | collective-permute-start | bytes 12296 | tf_op jit(solution)/shard_map/ppermute | solution.py:16
  138.0 10.8 %copy-start.34 = (f32[64,16]{0,1:T(8,128)}, f32[64,16]{0,1:T(8,128)S(1)}, u32[]{:S(2)}) copy-start(f32[64,16]{0,1:T(8,128)S(1)} %collective-permute-done.3) | copy-start | bytes 12292
  138.1 5.2 %collective-permute-start.4 = (f32[64,16]{0,1:T(8,128)S(1)}, f32[64,16]{0,1:T(8,128)S(1)}, u32[]{:S(2)}, u32[]{:S(2)}) collective-permute-start(f32[64,16]{0,1:T(8,128)S(1)} %convolution_add_fusion.13), channel_id=1, source_target_pairs={{0,16},{1,17},{2,18},{3,19},{4,20},{5,21},{6,22},{7,23},{8,24},{9,... | collective-permute-start | bytes 12296 | tf_op jit(solution)/shard_map/ppermute | solution.py:16
  143.3 5.6 %copy-start.35 = (f32[64,16]{0,1:T(8,128)}, f32[64,16]{0,1:T(8,128)S(1)}, u32[]{:S(2)}) copy-start(f32[64,16]{0,1:T(8,128)S(1)} %collective-permute-done.4) | copy-start | bytes 12292
  143.4 3.7 %collective-permute-start.5 = (f32[64,16]{0,1:T(8,128)S(1)}, f32[64,16]{0,1:T(8,128)S(1)}, u32[]{:S(2)}, u32[]{:S(2)}) collective-permute-start(f32[64,16]{0,1:T(8,128)S(1)} %convolution_add_fusion.11), channel_id=1, source_target_pairs={{0,32},{1,33},{2,34},{3,35},{4,36},{5,37},{6,38},{7,39},{8,40},{9,... | collective-permute-start | bytes 12296 | tf_op jit(solution)/shard_map/ppermute | solution.py:16
  147.1 1.8 copy-start.36
  147.8 57.6 %collective-permute-start.6 = (f32[64,16]{0,1:T(8,128)}, f32[64,16]{0,1:T(8,128)}, u32[]{:S(2)}, u32[]{:S(2)}) collective-permute-start(f32[64,16]{0,1:T(8,128)} %convolution_add_fusion.9), channel_id=1, source_target_pairs={{0,64},{1,65},{2,66},{3,67},{4,68},{5,69},{6,70},{7,71},{8,72},{9,... | collective-permute-start | bytes 12296 | tf_op jit(solution)/shard_map/ppermute | solution.py:16
  148.9 66.1 %copy-start.20 = (bf16[1,64,64]{2,1,0:T(8,128)(2,1)S(1)}, bf16[1,64,64]{2,1,0:T(8,128)(2,1)}, u32[]{:S(2)}) copy-start(bf16[1,64,64]{2,1,0:T(8,128)(2,1)} %copy-done.19) | copy-start | bytes 24580
  148.9 67.1 %copy-start.18 = (bf16[2,64,64]{2,1,0:T(8,128)(2,1)S(1)}, bf16[2,64,64]{2,1,0:T(8,128)(2,1)}, u32[]{:S(2)}) copy-start(bf16[2,64,64]{2,1,0:T(8,128)(2,1)} %copy.151) | copy-start | bytes 49156
  148.9 68.0 %copy-start.15 = (bf16[4,64,64]{2,1,0:T(8,128)(2,1)S(1)}, bf16[4,64,64]{2,1,0:T(8,128)(2,1)}, u32[]{:S(2)}) copy-start(bf16[4,64,64]{2,1,0:T(8,128)(2,1)} %copy.147) | copy-start | bytes 98308
  148.9 70.2 %copy-start.17 = (f32[16,16,64]{2,1,0:T(8,128)S(1)}, f32[16,16,64]{2,1,0:T(8,128)}, u32[]{:S(2)}) copy-start(f32[16,16,64]{2,1,0:T(8,128)} %fusion.43) | copy-start | bytes 196612
  148.9 70.8 %copy-start.8 = (bf16[32,64,64]{2,1,0:T(8,128)(2,1)S(1)}, bf16[32,64,64]{2,1,0:T(8,128)(2,1)}, u32[]{:S(2)}) copy-start(bf16[32,64,64]{2,1,0:T(8,128)(2,1)} %copy-done.7) | copy-start | bytes 786436
  224.7 4.9 %copy-start.30 = (pred[64,4]{1,0:T(8,128)(4,1)S(1)}, pred[64,4]{1,0:T(8,128)(4,1)}, u32[]{:S(2)}) copy-start(pred[64,4]{1,0:T(8,128)(4,1)} %copy.85) | copy-start | bytes 772
  224.7 4.9 %copy-start.31 = (pred[64,4]{1,0:T(8,128)(4,1)S(1)}, pred[64,4]{1,0:T(8,128)(4,1)}, u32[]{:S(2)}) copy-start(pred[64,4]{1,0:T(8,128)(4,1)} %copy.86) | copy-start | bytes 772
  229.7 10.4 %copy-start.5 = (bf16[64,64,64]{2,1,0:T(8,128)(2,1)S(1)}, bf16[64,64,64]{2,1,0:T(8,128)(2,1)}, u32[]{:S(2)}) copy-start(bf16[64,64,64]{2,1,0:T(8,128)(2,1)} %copy-done.4) | copy-start | bytes 1572868
Sparse Core Ops, SparseCore 0:
  43.8 26.0 all-gather.1
where the time goes:
time: 254 us; the launch traced here: 250 us
  local copies, waits for them, and re-layouts  103 us (41%)
  matrix products  83.7 us (33%)
  other arithmetic  21.5 us (8%)
  starting transfers between devices  16.3 us (6%)
  between operations  14.6 us (6%)
  waiting for transfers between devices  11.4 us (4%)
    unnamed x106, local copies, waits for them, and re-layouts  53.4 us
    dot_general x12, matrix products, near_step(): product = jnp.einsum('grj,gij->gri', picked, blocks, precision=highest)  24 us
    and x12, other arithmetic, near_step(): picked = jnp.take(extended, source_local, axis=0)  17 us
    dynamic_slice x2, local copies, waits for them, and re-layouts, pick_row(): lax.dynamic_index_in_dim(matrices, position, 0, keepdims=False)  12.4 us
    ppermute x7, waiting for transfers between devices, swapped_2(): return lax.ppermute(value, axis, pairs)  11.3 us
    ppermute x7, starting transfers between devices, swapped_2(): return lax.ppermute(value, axis, pairs)  10.5 us
    dot_general x1, matrix products, shards(): jnp.einsum('tjab,tjbr->tar', leaf_coupling.astype(jnp.float32), partner_c...  10.4 us
    dot_general x5, matrix products, couple(): jnp.einsum('cab,cbr->car', coupling.astype(jnp.float32), coefficients, pr...  9.95 us
  transfers between devices with their start and end apart: 10, of which 5 were waited for; matrix products, arithmetic and copies ran while one was open for 61% of the time, Pallas kernels for 0%

commit v1 on v0

v1 whole, which is shorter than its diff:
```python
import functools

import jax
import jax.numpy as jnp
from jax import lax
from jax.experimental import pallas as pl
from jax.experimental.pallas import tpu as pltpu
from jax.sharding import PartitionSpec as P

MESH = pl.DeviceIdType.MESH
F32 = jnp.float32
BF16 = jnp.bfloat16

RHS = 16
RANK = 64
LEAF = 128
LEAVES = 64
PAIRS = LEAVES // 2
PARTNERS = 4
SLOTS = 192
ROWS, COLS = 16, 8
CHUNKS = 4
PART = PAIRS // CHUNKS
HEIGHT = 6
NEAR_PARTS = 4


def dot_nn(a, b):
    return lax.dot_general(a, b, (((1,), (0,)), ((), ())), preferred_element_type=F32)


def dot_nt(a, b):
    return lax.dot_general(a, b, (((1,), (1,)), ((), ())), preferred_element_type=F32)


def split(x):
    high = x.astype(BF16)
    low = (x - high.astype(F32)).astype(BF16)
    return jnp.concatenate([high, low], axis=0)


def joined(o):
    half = o.shape[0] // 2
    return o[:half] + o[half:]


def level_offset(h):
    return 2 * LEAVES - 2 * (LEAVES >> h)


def lev_base(h):
    return PAIRS - (PAIRS >> (h - 1)) if h >= 1 else 0


def kernel(
    em_h, bs_h, bt_h, lt_h, ls_h, ut_h, us_h, lsrc, lc_h, nb_h, nt_v, nsrc, ncnt,
    out_h,
    em, bs, bt, lt, ls, ut, us, lc, nb,
    eh, halo, gath, dup, mp, mb, mu, eu, su, lev, sib, ylev, carried,
    xr, zr, upair, prod, nacc, cp, out,
    load_sem, nb_sem, bs_sem, out_sem, halo_s, halo_r,
    own_s, fwd_s, gath_r, xr_s, xr_r, zr_s, zr_r,
):
    row, col = lax.axis_index("row"), lax.axis_index("col")
    device = row * COLS + col
    z, core = col // 2, col % 2
    sibling = z * 2 + 1 - core
    znext = lax.rem(z + 1, 4)
    zprev = lax.rem(z + 3, 4)
    zfar = lax.rem(z + 2, 4)
    up_col, down_col, far_col = znext * 2 + core, zprev * 2 + core, zfar * 2 + core

    def load(src, dst, i):
        c = pltpu.make_async_copy(src, dst, load_sem.at[i])
        c.start()
        return c

    em_c = load(em_h, em, 0)
    width = 8192 // CHUNKS
    bs_c = []
    for k in range(CHUNKS):
        c = pltpu.make_async_copy(
            bs_h.at[:, pl.ds(k * width, width)], bs.at[:, pl.ds(k * width, width)], bs_sem.at[k]
        )
        c.start()
        bs_c.append(c)
    lt_c = load(lt_h, lt, 1)

    barrier = pltpu.get_barrier_semaphore()
    nxt, prv = lax.rem(device + 1, ROWS * COLS), lax.rem(device + ROWS * COLS - 1, ROWS * COLS)
    next_id = (nxt // COLS, lax.rem(nxt, COLS))
    prev_id = (prv // COLS, lax.rem(prv, COLS))
    for i in range(1, COLS):
        pl.semaphore_signal(barrier, 1, device_id=(row, lax.rem(col + i, COLS)), device_id_type=MESH)
    for i in range(1, ROWS):
        pl.semaphore_signal(barrier, 1, device_id=(lax.rem(row + i, ROWS), col), device_id_type=MESH)
    pl.semaphore_signal(barrier, 1, device_id=next_id, device_id_type=MESH)
    pl.semaphore_signal(barrier, 1, device_id=prev_id, device_id_type=MESH)

    ut_c = load(ut_h, ut, 2)
    us_c = load(us_h, us, 3)
    ls_c = load(ls_h, ls, 4)
    nb_c = []
    per = SLOTS // NEAR_PARTS
    for k in range(NEAR_PARTS):
        c = pltpu.make_async_copy(
            nb_h.at[pl.ds(k * per, per)], nb.at[pl.ds(k * per, per)], nb_sem.at[k]
        )
        c.start()
        nb_c.append(c)
    lc_c = load(lc_h, lc, 5)
    bt_c = load(bt_h, bt, 6)

    lane = lax.broadcasted_iota(jnp.int32, (RHS, 128), 1)
    first_half = lane < 64
    lane2 = lax.broadcasted_iota(jnp.int32, (2 * RHS, 128), 1)
    first_half2 = lane2 < 64

    em_c.wait()

    def split_leaf(g, carry):
        for u in range(8):
            l = g * 8 + u
            eh[l + 1] = split(em[:, pl.ds(pl.multiple_of(l * LEAF, LEAF), LEAF)])
        return carry

    lax.fori_loop(0, LEAVES // 8, split_leaf, 0)

    pl.semaphore_wait(barrier, COLS - 1 + ROWS - 1 + 2)

    halo_next = pltpu.make_async_remote_copy(
        em.at[:, pl.ds((LEAVES - 1) * LEAF, LEAF)], halo.at[0], halo_s.at[0], halo_r.at[0],
        device_id=next_id, device_id_type=MESH)
    halo_prev = pltpu.make_async_remote_copy(
        em.at[:, pl.ds(0, LEAF)], halo.at[1], halo_s.at[1], halo_r.at[1],
        device_id=prev_id, device_id_type=MESH)
    halo_next.start()
    halo_prev.start()

    def piece(owner, k):
        return gath.at[owner, pl.ds(k * PART, PART)]

    def send(owner, k, to_col, send_sem, kind):
        return pltpu.make_async_remote_copy(
            piece(owner, k), piece(owner, k), send_sem, gath_r.at[kind, k],
            device_id=(row, to_col), device_id_type=MESH)

    sends = []

    def leaf_pair(p):
        a = eh[pl.ds(2 * p + 1, 2)].reshape(64, 128)
        start = pl.multiple_of(p * 256, 256)
        w = bs[:, pl.ds(start, 256)]
        b = jnp.concatenate([w[:, :128], w[:, 128:]], axis=0)
        o = dot_nt(a, b)
        gath[col, p] = jnp.where(first_half, o[0:16] + o[16:32], o[32:48] + o[48:64])

    for k in range(CHUNKS):
        bs_c[k].wait()

        def leaf_step(g, carry, k=k):
            for u in range(4):
                leaf_pair(k * PART + g * 4 + u)
            return carry

        lax.fori_loop(0, PART // 4, leaf_step, 0)
        for n, (to_col, kind) in enumerate(((up_col, 1), (down_col, 2), (sibling, 0))):
            c = send(col, k, to_col, own_s.at[n, k], kind)
            c.start()
            sends.append(c)

    lt_c.wait()
    eye = (
        lax.broadcasted_iota(jnp.int32, (128, 126), 0)
        == lax.broadcasted_iota(jnp.int32, (128, 126), 1)
    ).astype(BF16)

    def turn_local(q, carry):
        w = jnp.concatenate([lt[q], lt[q + 32]], axis=0)
        mp[pl.ds(q, 128, stride=32), :] = dot_nt(eye, w)
        return carry

    lax.fori_loop(0, 32, turn_local, 0, unroll=2)

    def unpack(source, target, n):
        m = source[pl.ds(pl.multiple_of(n * 32, 32), 32), :].astype(BF16)
        target[n] = jnp.concatenate([m[:, :64], m[:, 64:]], axis=0)

    def unpack_local(g, carry):
        for u in range(6):
            unpack(mp, mb, g * 6 + u)
        return carry

    lax.fori_loop(0, 21, unpack_local, 0)

    def lift(pair, weights):
        return joined(dot_nn(split(pair), weights.reshape(128, 64)))

    def level_pair(h, p):
        return gath[col, p] if h == 0 else lev[lev_base(h) + p]

    for h in range(HEIGHT - 1):
        count = PAIRS >> h
        off = level_offset(h)

        def up_two(q, h=h, off=off):
            one = lift(level_pair(h, 2 * q), mb[pl.ds(off + 4 * q, 2)])
            two = lift(level_pair(h, 2 * q + 1), mb[pl.ds(off + 4 * q + 2, 2)])
            lev[lev_base(h + 1) + q] = jnp.concatenate([one, two], axis=1)

        half = count // 2
        group = min(half, 4)

        def up_step(g, carry, up_two=up_two, group=group):
            for u in range(group):
                up_two(g * group + u)
            return carry

        lax.fori_loop(0, half // group, up_step, 0)
    root = lift(lev[lev_base(5)], mb[pl.ds(level_offset(5), 2)])

    def placed(value, parity):
        return jnp.where(
            (lane >= 64).astype(jnp.int32) == parity, jnp.concatenate([value, value], axis=1), 0.0
        )

    xr[col] = placed(root, core)
    xr_copies = []
    for i in range(1, COLS):
        c = pltpu.make_async_remote_copy(
            xr.at[col], xr.at[col], xr_s.at[i], xr_r.at[i],
            device_id=(row, lax.rem(col + i, COLS)), device_id_type=MESH)
        c.start()
        xr_copies.append(c)

    def recv(owner, k, kind):
        pltpu.make_async_remote_copy(
            piece(owner, k), piece(owner, k), own_s.at[0, k], gath_r.at[kind, k],
            device_id=(row, col), device_id_type=MESH).wait_recv()

    def relay_near(k):
        recv(down_col, k, 1)
        if k < CHUNKS // 2:
            c = send(down_col, k, up_col, fwd_s.at[0, k], 3)
            c.start()
            sends.append(c)
        c = send(down_col, k, sibling, fwd_s.at[1, k], 4)
        c.start()
        sends.append(c)
        recv(up_col, k, 2)
        if k >= CHUNKS // 2:
            c = send(up_col, k, down_col, fwd_s.at[0, k], 3)
            c.start()
            sends.append(c)
        c = send(up_col, k, sibling, fwd_s.at[2, k], 5)
        c.start()
        sends.append(c)

    def relay_far(k):
        recv(far_col, k, 3)
        c = send(far_col, k, sibling, fwd_s.at[3, k], 6)
        c.start()
        sends.append(c)

    ut_c.wait()
    us_c.wait()
    picks = lax.broadcasted_iota(jnp.int32, (64, 254), 0)
    cluster = lax.broadcasted_iota(jnp.int32, (64, 254), 1)
    want = jnp.where(picks < 8, row * 8 + picks, -1)
    want = jnp.where((picks >= 8) & (picks < 12), 128 + row * 4 + picks - 8, want)
    want = jnp.where((picks >= 12) & (picks < 14), 192 + row * 2 + picks - 12, want)
    want = jnp.where((picks >= 16) & (picks < 46), 224 + picks - 16, want)
    for j in range(7):
        want = jnp.where(picks == 48 + j, 256 - (256 >> j) + (device // (1 << j)), want)
    pick_u = (cluster == want).astype(BF16)
    picks_s = lax.broadcasted_iota(jnp.int32, (16, 254), 0)
    cluster_s = lax.broadcasted_iota(jnp.int32, (16, 254), 1)
    want_s = jnp.full((16, 254), -1, jnp.int32)
    for j in range(7):
        want_s = jnp.where(picks_s == j, 256 - (256 >> j) + (device // (1 << j)), want_s)
    pick_s = (cluster_s == want_s).astype(BF16)

    def turn_upper(q, carry):
        w = jnp.concatenate([ut[q], ut[q + 32]], axis=0)
        mu[pl.ds(q, 64, stride=32), :] = dot_nt(pick_u, w)
        return carry

    lax.fori_loop(0, 32, turn_upper, 0, unroll=2)

    def unpack_upper(g, carry):
        for u in range(8):
            unpack(mu, eu, g * 8 + u)
        return carry

    lax.fori_loop(0, 8, unpack_upper, 0)

    def turn_sib(q, carry):
        w = jnp.concatenate([us[q], us[q + 32]], axis=0)
        mp[pl.ds(q, 16, stride=32), :] = dot_nt(pick_s, w)
        return carry

    lax.fori_loop(0, 32, turn_sib, 0, unroll=2)

    def unpack_sib(g, carry):
        for u in range(8):
            unpack(mp, su, g * 8 + u)
        return carry

    lax.fori_loop(0, 1, unpack_sib, 0)

    relay_near(0)

    for i in range(1, COLS):
        peer = lax.rem(col + COLS - i, COLS)
        pltpu.make_async_remote_copy(
            xr.at[peer], xr.at[peer], xr_s.at[i], xr_r.at[i],
            device_id=(row, peer), device_id_type=MESH).wait_recv()
    for i in range(4):
        upair[i] = xr[2 * i] + xr[2 * i + 1]

    def up_upper(source, count, target, first):
        for i in range(count // 2):
            one = lift(upair[source + 2 * i], eu[first + 4 * i : first + 4 * i + 2])
            two = lift(upair[source + 2 * i + 1], eu[first + 4 * i + 2 : first + 4 * i + 4])
            upair[target + i] = jnp.concatenate([one, two], axis=1)

    up_upper(0, 4, 4, 0)
    up_upper(4, 2, 6, 8)
    row_root = lift(upair[6], eu[12:14])
    zr[row] = placed(row_root, lax.rem(row, 2))
    zr_copies = []
    for i in range(1, ROWS):
        c = pltpu.make_async_remote_copy(
            zr.at[row], zr.at[row], zr_s.at[i], zr_r.at[i],
            device_id=(lax.rem(row + i, ROWS), col), device_id_type=MESH)
        c.start()
        zr_copies.append(c)

    relay_near(1)

    halo_next.wait_recv()
    halo_prev.wait_recv()
    eh[0] = split(halo[0])
    eh[LEAVES + 1] = split(halo[1])
    leaf_first = device * LEAVES

    def near_part(k):
        nb_c[k].wait()

        def near_step(g, carry):
            for u in range(4):
                s = k * per + g * 4 + u
                source = jnp.clip(nsrc[s] - leaf_first + 1, 0, LEAVES + 1)
                o = dot_nt(eh[source], nb[s])
                prod[pl.ds(s, RHS, stride=SLOTS), :] = joined(o)
            return carry

        lax.fori_loop(0, per // 4, near_step, 0)

    near_part(0)
    near_part(1)
    relay_near(2)
    near_part(2)

    ls_c.wait()
    for h in range(1, HEIGHT):
        count = PAIRS >> h

        def sib_one(p, h=h):
            x = lev[lev_base(h) + p]
            lhs = jnp.concatenate([split(x[:, 64:]), split(x[:, :64])], axis=0)
            w = ls[pl.ds(LEAVES - 2 * (LEAVES >> h) + 2 * p, 2)].reshape(128, 64)
            o = dot_nt(lhs, w)
            sib[lev_base(h) + p] = jnp.where(first_half, o[0:16] + o[16:32], o[32:48] + o[48:64])

        group = min(count, 4)

        def sib_step(g, carry, sib_one=sib_one, group=group):
            for u in range(group):
                sib_one(g * group + u)
            return carry

        lax.fori_loop(0, count // group, sib_step, 0)

    relay_near(3)

    for i in range(1, ROWS):
        peer = lax.rem(row + ROWS - i, ROWS)
        pltpu.make_async_remote_copy(
            zr.at[peer], zr.at[peer], zr_s.at[i], zr_r.at[i],
            device_id=(peer, col), device_id_type=MESH).wait_recv()
    for i in range(8):
        upair[7 + i] = zr[2 * i] + zr[2 * i + 1]
    up_upper(7, 8, 15, 16)
    up_upper(15, 4, 19, 32)
    up_upper(19, 2, 21, 40)

    own = []
    for j, base in enumerate((0, 4, 6, 7, 15, 19, 21)):
        own.append((base, col // (1 << j)) if j < 3 else (base, row // (1 << (j - 3))))
    y = jnp.zeros((RHS, RANK), F32)
    for j in range(6, -1, -1):
        base, mine = own[j]
        pair = upair[base + mine // 2]
        turned = jnp.concatenate([pair[:, 64:], pair[:, :64]], axis=1)
        other = jnp.where(lax.rem(mine, 2) == 1, pair, turned)[:, :64]
        y = joined(dot_nt(split(other), su[j])) + joined(dot_nt(split(y), eu[48 + j]))

    ylev[30] = placed(y, 0)
    for h in range(HEIGHT - 1, -1, -1):
        count = PAIRS >> h
        off = level_offset(h)

        def down_one(parent, p, h=h, off=off):
            w = mb[pl.ds(off + 2 * p, 2)].reshape(128, 64)
            value = joined(dot_nt(split(parent), w))
            if h:
                ylev[lev_base(h) + p] = value + sib[lev_base(h) + p]
            else:
                carried[p] = value

        if h == HEIGHT - 1:
            down_one(y, 0)
            continue

        def down_two(q, h=h, down_one=down_one):
            pair = ylev[lev_base(h + 1) + q]
            down_one(pair[:, :64], 2 * q)
            down_one(pair[:, 64:], 2 * q + 1)

        half = count // 2
        group = min(half, 4)

        def down_step(g, carry, down_two=down_two, group=group):
            for u in range(group):
                down_two(g * group + u)
            return carry

        lax.fori_loop(0, half // group, down_step, 0)

    lc_c.wait()

    def pack_leaf(g, carry):
        for u in range(4):
            t = g * 4 + u
            cp[t] = jnp.concatenate([lc[t, 0], lc[t, 1], lc[t, 2], lc[t, 3]], axis=1)
        return carry

    lax.fori_loop(0, LEAVES // 4, pack_leaf, 0)

    near_part(3)

    target = nt_v[...] - leaf_first
    slot = lax.broadcasted_iota(jnp.int32, (LEAVES, SLOTS), 1)
    one_hot = (
        (jnp.broadcast_to(target, (LEAVES, SLOTS))
         == lax.broadcasted_iota(jnp.int32, (LEAVES, SLOTS), 0))
        & (slot < ncnt[0])
    ).astype(BF16)

    def sum_step(g, carry):
        for u in range(2):
            r = g * 2 + u
            x = prod[pl.ds(pl.multiple_of(r * SLOTS, SLOTS), SLOTS), :]
            high = x.astype(BF16)
            low = (x - high.astype(F32)).astype(BF16)
            nacc[pl.ds(r, LEAVES, stride=RHS), :] = dot_nn(one_hot, high) + dot_nn(one_hot, low)
        return carry

    lax.fori_loop(0, RHS // 2, sum_step, 0)

    def dup_part(owner, k):
        def dup_step(g, carry):
            for u in range(4):
                p = k * PART + g * 4 + u
                x = gath[owner, p]
                turned = jnp.concatenate([x[:, 64:], x[:, :64]], axis=1)
                base = owner * LEAVES + 2 * p
                dup[base] = split(jnp.where(first_half, x, turned))
                dup[base + 1] = split(jnp.where(first_half, turned, x))
            return carry

        lax.fori_loop(0, PART // 4, dup_step, 0)

    for k in range(CHUNKS):
        relay_far(k)
    other = 1 - core
    for k in range(CHUNKS):
        dup_part(col, k)
        dup_part(down_col, k)
        dup_part(up_col, k)
        recv(sibling, k, 0)
        dup_part(sibling, k)
        recv(zprev * 2 + other, k, 4)
        dup_part(zprev * 2 + other, k)
        recv(znext * 2 + other, k, 5)
        dup_part(znext * 2 + other, k)
    for k in range(CHUNKS):
        dup_part(far_col, k)
        recv(zfar * 2 + other, k, 6)
        dup_part(zfar * 2 + other, k)

    bt_c.wait()
    group_first = row * (LEAVES * COLS)

    def final_leaf(t, q, u):
        d = [dup[jnp.clip(lsrc[j, t] - group_first, 0, LEAVES * COLS - 1)] for j in range(PARTNERS)]
        lhs = jnp.concatenate(
            [jnp.where(first_half2, d[0], d[1]), jnp.where(first_half2, d[2], d[3])], axis=1)
        c = carried[q]
        c = c[:, :64] if u == 0 else c[:, 64:]
        y0 = joined(dot_nt(lhs, cp[t])) + c
        start = pl.multiple_of(t * LEAF, LEAF)
        far = joined(dot_nn(split(y0), bt[:, pl.ds(start, LEAF)]))
        out[:, pl.ds(start, LEAF)] = far + nacc[pl.ds(pl.multiple_of(t * RHS, RHS), RHS), :]

    def final_step(g, carry):
        for u in range(4):
            q = g * 4 + u
            final_leaf(2 * q, q, 0)
            final_leaf(2 * q + 1, q, 1)
        return carry

    lax.fori_loop(0, PAIRS // 4, final_step, 0)
    out_c = pltpu.make_async_copy(out, out_h, out_sem)
    out_c.start()
    halo_next.wait_send()
    halo_prev.wait_send()
    for c in sends + xr_copies + zr_copies:
        c.wait_send()
    out_c.wait()


def shards(
    emission, basis_source, basis_target, local_transfer, local_sibling, upper_transfer,
    upper_sibling, leaf_source, leaf_coupling, near_block, near_target, near_source, near_count,
):
    hbm = pl.BlockSpec(memory_space=pl.ANY)
    smem = pl.BlockSpec(memory_space=pltpu.SMEM)
    vmem = pl.BlockSpec(memory_space=pltpu.VMEM)
    dma = pltpu.SemaphoreType.DMA
    V = pltpu.VMEM
    return pl.pallas_call(
        kernel,
        out_shape=jax.ShapeDtypeStruct((RHS, LEAVES * LEAF), F32),
        in_specs=[hbm] * 7 + [smem, hbm, hbm, vmem, smem, smem],
        out_specs=hbm,
        scratch_shapes=[
            V((RHS, 8192), F32), V((RANK, 8192), BF16), V((RANK, 8192), BF16),
            V((64, 64, 126), BF16), V((62, 64, 64), BF16),
            V((64, 64, 254), BF16), V((64, 64, 254), BF16),
            V((LEAVES, PARTNERS, 64, 64), BF16), V((SLOTS, 128, 128), BF16),
            V((LEAVES + 2, 32, 128), BF16),
            V((2, RHS, 128), F32),
            V((COLS, PAIRS, RHS, 128), F32),
            V((COLS * LEAVES, 32, 128), BF16),
            V((128 * 32, 128), F32),
            V((126, 64, 64), BF16),
            V((64 * 32, 128), F32),
            V((64, 64, 64), BF16),
            V((8, 64, 64), BF16),
            V((32, RHS, 128), F32),
            V((32, RHS, 128), F32),
            V((32, RHS, 128), F32),
            V((PAIRS, RHS, 128), F32),
            V((COLS, RHS, 128), F32),
            V((ROWS, RHS, 128), F32),
            V((22, RHS, 128), F32),
            V((RHS * SLOTS, 128), F32),
            V((LEAVES * RHS, 128), F32),
            V((LEAVES, 64, 256), BF16),
            V((RHS, 8192), F32),
            dma((7,)), dma((NEAR_PARTS,)), dma((CHUNKS,)), dma, dma((2,)), dma((2,)),
            dma((3, CHUNKS)), dma((4, CHUNKS)), dma((7, CHUNKS)),
            dma((COLS,)), dma((COLS,)), dma((ROWS,)), dma((ROWS,)),
        ],
        compiler_params=pltpu.CompilerParams(
            collective_id=0, has_side_effects=True, vmem_limit_bytes=58 * 1024 * 1024),
        name="h2_product",
    )(
        emission, basis_source, basis_target, local_transfer.transpose(1, 2, 0), local_sibling,
        upper_transfer.transpose(1, 2, 0), upper_sibling.transpose(1, 2, 0), leaf_source.T,
        leaf_coupling, near_block, near_target.reshape(1, SLOTS), near_source, near_count,
    )


def solution(mesh):
    both = ("row", "col")
    in_specs = (
        P(None, both), P(None, both), P(None, both), P(both, None, None), P(both, None, None),
        P(), P(), P(both, None), P(both, None, None, None), P(both, None, None),
        P(both), P(both), P(both),
    )
    return jax.shard_map(
        shards, mesh=mesh, in_specs=in_specs, out_specs=P(None, both), check_vma=False)
```

time: 254 us -> 66.8 us (0.26)
  the two profiles are of different devices: /device:TPU:88 before, /device:TPU:0 now
where the time goes in v1:
time: 66.8 us; the launch traced here: 66.6 us
  Pallas kernels  64.1 us (96%)
  local copies, waits for them, and re-layouts  1.87 us (3%)
    pallas_call x1, Pallas kernels, shards(): pl.pallas_call(kernel, out_shape=jax.ShapeDtypeStruct((RHS, LEAVES * LEAF...  64.1 us
    unnamed x1, local copies, waits for them, and re-layouts  1.87 us

profile of v1, /device:TPU:0, one launch (start us, length us, event | category | flops | bytes accessed | tf_op | source)
XLA Modules:
  0.0 66.6 jit_solution(11429124180011818768)
XLA Ops:
  0.7 64.1 %h2_product.1 = f32[16,8192]{1,0:T(8,128)} custom-call(f32[16,8192]{1,0:T(8,128)} %em_h.1, bf16[64,8192]{1,0:T(8,128)(2,1)} %bs_h.1, bf16[64,8192]{1,0:T(8,128)(2,1)} %bt_h.1, bf16[64,64,126]{2,1,0:T(8,128)(2,1)} %bitcast.7, bf16[62,64,64]{2,1,0:T(8,128)(2,1)} %ls_h.1, bf16[64,64,254]{2,1,0:T(8,128)(2,1)} %bitcast.5, bf16[64,64,254]{2,1,0:T(8,128)(2,1)} %bitcast.6, ...), custom_call_target="tpu_custom_call" | custom-call | tf_op jit(solution)/shard_map/h2_product/pallas_call | solution.py:543
  64.7 1.9 %copy.16 = f32[16,8192]{1,0:T(8,128)} copy(f32[16,8192]{1,0:T(8,128)} %h2_product.1) | data formatting | bytes 1048576

commit v2 on v1

--- a/solution.py
+++ b/solution.py
@@ -23,6 +23,7 @@
 PART = PAIRS // CHUNKS
 HEIGHT = 6
 NEAR_PARTS = 4
+FINAL = 16
 
 
 def dot_nn(a, b):
@@ -159,11 +160,11 @@
         bs_c[k].wait()
 
         def leaf_step(g, carry, k=k):
-            for u in range(4):
-                leaf_pair(k * PART + g * 4 + u)
+            for u in range(8):
+                leaf_pair(k * PART + g * 8 + u)
             return carry
 
-        lax.fori_loop(0, PART // 4, leaf_step, 0)
+        lax.fori_loop(0, PART // 8, leaf_step, 0)
         for n, (to_col, kind) in enumerate(((up_col, 1), (down_col, 2), (sibling, 0))):
             c = send(col, k, to_col, own_s.at[n, k], kind)
             c.start()
@@ -180,18 +181,18 @@
         mp[pl.ds(q, 128, stride=32), :] = dot_nt(eye, w)
         return carry
 
-    lax.fori_loop(0, 32, turn_local, 0, unroll=2)
+    lax.fori_loop(0, 32, turn_local, 0, unroll=4)
 
     def unpack(source, target, n):
         m = source[pl.ds(pl.multiple_of(n * 32, 32), 32), :].astype(BF16)
         target[n] = jnp.concatenate([m[:, :64], m[:, 64:]], axis=0)
 
     def unpack_local(g, carry):
-        for u in range(6):
-            unpack(mp, mb, g * 6 + u)
-        return carry
-
-    lax.fori_loop(0, 21, unpack_local, 0)
+        for u in range(18):
+            unpack(mp, mb, g * 18 + u)
+        return carry
+
+    lax.fori_loop(0, 7, unpack_local, 0)
 
     def lift(pair, weights):
         return joined(dot_nn(split(pair), weights.reshape(128, 64)))
@@ -209,7 +210,7 @@
             lev[lev_base(h + 1) + q] = jnp.concatenate([one, two], axis=1)
 
         half = count // 2
-        group = min(half, 4)
+        group = min(half, 8)
 
         def up_step(g, carry, up_two=up_two, group=group):
             for u in range(group):
@@ -283,30 +284,20 @@
     def turn_upper(q, carry):
         w = jnp.concatenate([ut[q], ut[q + 32]], axis=0)
         mu[pl.ds(q, 64, stride=32), :] = dot_nt(pick_u, w)
-        return carry
-
-    lax.fori_loop(0, 32, turn_upper, 0, unroll=2)
-
-    def unpack_upper(g, carry):
-        for u in range(8):
-            unpack(mu, eu, g * 8 + u)
-        return carry
-
-    lax.fori_loop(0, 8, unpack_upper, 0)
-
-    def turn_sib(q, carry):
         w = jnp.concatenate([us[q], us[q + 32]], axis=0)
         mp[pl.ds(q, 16, stride=32), :] = dot_nt(pick_s, w)
         return carry
 
-    lax.fori_loop(0, 32, turn_sib, 0, unroll=2)
-
-    def unpack_sib(g, carry):
-        for u in range(8):
-            unpack(mp, su, g * 8 + u)
-        return carry
-
-    lax.fori_loop(0, 1, unpack_sib, 0)
+    lax.fori_loop(0, 32, turn_upper, 0, unroll=4)
+
+    def unpack_upper(g, carry):
+        for u in range(16):
+            unpack(mu, eu, g * 16 + u)
+        for u in range(2):
+            unpack(mp, su, g * 2 + u)
+        return carry
+
+    lax.fori_loop(0, 4, unpack_upper, 0)
 
     relay_near(0)
 
@@ -348,14 +339,14 @@
         nb_c[k].wait()
 
         def near_step(g, carry):
-            for u in range(4):
-                s = k * per + g * 4 + u
+            for u in range(16):
+                s = k * per + g * 16 + u
                 source = jnp.clip(nsrc[s] - leaf_first + 1, 0, LEAVES + 1)
                 o = dot_nt(eh[source], nb[s])
                 prod[pl.ds(s, RHS, stride=SLOTS), :] = joined(o)
             return carry
 
-        lax.fori_loop(0, per // 4, near_step, 0)
+        lax.fori_loop(0, per // 16, near_step, 0)
 
     near_part(0)
     near_part(1)
@@ -373,7 +364,7 @@
             o = dot_nt(lhs, w)
             sib[lev_base(h) + p] = jnp.where(first_half, o[0:16] + o[16:32], o[32:48] + o[48:64])
 
-        group = min(count, 4)
+        group = min(count, 8)
 
         def sib_step(g, carry, sib_one=sib_one, group=group):
             for u in range(group):
@@ -429,7 +420,7 @@
             down_one(pair[:, 64:], 2 * q + 1)
 
         half = count // 2
-        group = min(half, 4)
+        group = min(half, 8)
 
         def down_step(g, carry, down_two=down_two, group=group):
             for u in range(group):
@@ -441,12 +432,12 @@
     lc_c.wait()
 
     def pack_leaf(g, carry):
-        for u in range(4):
-            t = g * 4 + u
+        for u in range(16):
+            t = g * 16 + u
             cp[t] = jnp.concatenate([lc[t, 0], lc[t, 1], lc[t, 2], lc[t, 3]], axis=1)
         return carry
 
-    lax.fori_loop(0, LEAVES // 4, pack_leaf, 0)
+    lax.fori_loop(0, LEAVES // 16, pack_leaf, 0)
 
     near_part(3)
 
@@ -459,20 +450,20 @@
     ).astype(BF16)
 
     def sum_step(g, carry):
-        for u in range(2):
-            r = g * 2 + u
+        for u in range(4):
+            r = g * 4 + u
             x = prod[pl.ds(pl.multiple_of(r * SLOTS, SLOTS), SLOTS), :]
             high = x.astype(BF16)
             low = (x - high.astype(F32)).astype(BF16)
             nacc[pl.ds(r, LEAVES, stride=RHS), :] = dot_nn(one_hot, high) + dot_nn(one_hot, low)
         return carry
 
-    lax.fori_loop(0, RHS // 2, sum_step, 0)
+    lax.fori_loop(0, RHS // 4, sum_step, 0)
 
     def dup_part(owner, k):
         def dup_step(g, carry):
-            for u in range(4):
-                p = k * PART + g * 4 + u
+            for u in range(8):
+                p = k * PART + g * 8 + u
                 x = gath[owner, p]
                 turned = jnp.concatenate([x[:, 64:], x[:, :64]], axis=1)
                 base = owner * LEAVES + 2 * p
@@ -480,7 +471,7 @@
                 dup[base + 1] = split(jnp.where(first_half, turned, x))
             return carry
 
-        lax.fori_loop(0, PART // 4, dup_step, 0)
+        lax.fori_loop(0, PART // 8, dup_step, 0)
 
     for k in range(CHUNKS):
         relay_far(k)
@@ -503,25 +494,27 @@
     bt_c.wait()
     group_first = row * (LEAVES * COLS)
 
-    def final_leaf(t, q, u):
-        d = [dup[jnp.clip(lsrc[j, t] - group_first, 0, LEAVES * COLS - 1)] for j in range(PARTNERS)]
-        lhs = jnp.concatenate(
-            [jnp.where(first_half2, d[0], d[1]), jnp.where(first_half2, d[2], d[3])], axis=1)
-        c = carried[q]
-        c = c[:, :64] if u == 0 else c[:, 64:]
-        y0 = joined(dot_nt(lhs, cp[t])) + c
-        start = pl.multiple_of(t * LEAF, LEAF)
-        far = joined(dot_nn(split(y0), bt[:, pl.ds(start, LEAF)]))
-        out[:, pl.ds(start, LEAF)] = far + nacc[pl.ds(pl.multiple_of(t * RHS, RHS), RHS), :]
-
     def final_step(g, carry):
-        for u in range(4):
-            q = g * 4 + u
-            final_leaf(2 * q, q, 0)
-            final_leaf(2 * q + 1, q, 1)
-        return carry
-
-    lax.fori_loop(0, PAIRS // 4, final_step, 0)
+        leaves = [g * FINAL + u for u in range(FINAL)]
+        lhs = []
+        for t in leaves:
+            d = [dup[jnp.clip(lsrc[j, t] - group_first, 0, LEAVES * COLS - 1)]
+                 for j in range(PARTNERS)]
+            lhs.append(jnp.concatenate(
+                [jnp.where(first_half2, d[0], d[1]), jnp.where(first_half2, d[2], d[3])], axis=1))
+        listed = [dot_nt(x, cp[t]) for x, t in zip(lhs, leaves)]
+        y0 = []
+        for u, o in enumerate(listed):
+            c = carried[g * (FINAL // 2) + u // 2]
+            y0.append(split(joined(o) + (c[:, :64] if u % 2 == 0 else c[:, 64:])))
+        starts = [pl.multiple_of(t * LEAF, LEAF) for t in leaves]
+        far = [dot_nn(y, bt[:, pl.ds(start, LEAF)]) for y, start in zip(y0, starts)]
+        for o, t, start in zip(far, leaves, starts):
+            near = nacc[pl.ds(pl.multiple_of(t * RHS, RHS), RHS), :]
+            out[:, pl.ds(start, LEAF)] = joined(o) + near
+        return carry
+
+    lax.fori_loop(0, LEAVES // FINAL, final_step, 0)
     out_c = pltpu.make_async_copy(out, out_h, out_sem)
     out_c.start()
     halo_next.wait_send()

time: 66.8 us -> 40.4 us (0.60)
  the two profiles are of different devices: /device:TPU:0 before, /device:TPU:1 now
where the time goes in v2:
time: 40.4 us; the launch traced here: 40.2 us
  Pallas kernels  37.7 us (93%)
  local copies, waits for them, and re-layouts  1.87 us (5%)
  between operations  0.66 us (2%)
    pallas_call x1, Pallas kernels, shards(): pl.pallas_call(kernel, out_shape=jax.ShapeDtypeStruct((RHS, LEAVES * LEAF...  37.7 us
    unnamed x1, local copies, waits for them, and re-layouts  1.87 us

profile of v2, /device:TPU:1, one launch (start us, length us, event | category | flops | bytes accessed | tf_op | source)
XLA Modules:
  0.0 40.2 jit_solution(8258548448360806986)
XLA Ops:
  0.7 37.7 %h2_product.1 = f32[16,8192]{1,0:T(8,128)} custom-call(f32[16,8192]{1,0:T(8,128)} %em_h.1, bf16[64,8192]{1,0:T(8,128)(2,1)} %bs_h.1, bf16[64,8192]{1,0:T(8,128)(2,1)} %bt_h.1, bf16[64,64,126]{2,1,0:T(8,128)(2,1)} %bitcast.7, bf16[62,64,64]{2,1,0:T(8,128)(2,1)} %ls_h.1, bf16[64,64,254]{2,1,0:T(8,128)(2,1)} %bitcast.5, bf16[64,64,254]{2,1,0:T(8,128)(2,1)} %bitcast.6, ...), custom_call_target="tpu_custom_call" | custom-call | tf_op jit(solution)/shard_map/h2_product/pallas_call | solution.py:536
  38.3 1.9 %copy.16 = f32[16,8192]{1,0:T(8,128)} copy(f32[16,8192]{1,0:T(8,128)} %h2_product.1) | data formatting | bytes 1048576

commit v3 on v2

--- a/solution.py
+++ b/solution.py
@@ -24,6 +24,7 @@
 HEIGHT = 6
 NEAR_PARTS = 4
 FINAL = 16
+MAT, SLOT_ROWS, LEAF_ROWS = 33, SLOTS + 1, RHS + 1
 
 
 def dot_nn(a, b):
@@ -59,7 +60,7 @@
     em, bs, bt, lt, ls, ut, us, lc, nb,
     eh, halo, gath, dup, mp, mb, mu, eu, su, lev, sib, ylev, carried,
     xr, zr, upair, prod, nacc, cp, out,
-    load_sem, nb_sem, bs_sem, out_sem, halo_s, halo_r,
+    load_sem, nb_sem, lc_sem, bs_sem, out_sem, halo_s, halo_r,
     own_s, fwd_s, gath_r, xr_s, xr_r, zr_s, zr_r,
 ):
     row, col = lax.axis_index("row"), lax.axis_index("col")
@@ -85,7 +86,6 @@
         )
         c.start()
         bs_c.append(c)
-    lt_c = load(lt_h, lt, 1)
 
     barrier = pltpu.get_barrier_semaphore()
     nxt, prv = lax.rem(device + 1, ROWS * COLS), lax.rem(device + ROWS * COLS - 1, ROWS * COLS)
@@ -98,19 +98,13 @@
     pl.semaphore_signal(barrier, 1, device_id=next_id, device_id_type=MESH)
     pl.semaphore_signal(barrier, 1, device_id=prev_id, device_id_type=MESH)
 
-    ut_c = load(ut_h, ut, 2)
-    us_c = load(us_h, us, 3)
-    ls_c = load(ls_h, ls, 4)
-    nb_c = []
-    per = SLOTS // NEAR_PARTS
-    for k in range(NEAR_PARTS):
-        c = pltpu.make_async_copy(
-            nb_h.at[pl.ds(k * per, per)], nb.at[pl.ds(k * per, per)], nb_sem.at[k]
-        )
-        c.start()
-        nb_c.append(c)
-    lc_c = load(lc_h, lc, 5)
-    bt_c = load(bt_h, bt, 6)
+    per, lper = SLOTS // NEAR_PARTS, LEAVES // NEAR_PARTS
+
+    def load_near(k):
+        pltpu.make_async_copy(
+            nb_h.at[pl.ds(k * per, per)], nb.at[pl.ds(k * per, per)], nb_sem.at[k]).start()
+        pltpu.make_async_copy(
+            lc_h.at[pl.ds(k * lper, lper)], lc.at[pl.ds(k * lper, lper)], lc_sem.at[k]).start()
 
     lane = lax.broadcasted_iota(jnp.int32, (RHS, 128), 1)
     first_half = lane < 64
@@ -118,6 +112,7 @@
     first_half2 = lane2 < 64
 
     em_c.wait()
+    lt_c = load(lt_h, lt, 1)
 
     def split_leaf(g, carry):
         for u in range(8):
@@ -169,70 +164,6 @@
             c = send(col, k, to_col, own_s.at[n, k], kind)
             c.start()
             sends.append(c)
-
-    lt_c.wait()
-    eye = (
-        lax.broadcasted_iota(jnp.int32, (128, 126), 0)
-        == lax.broadcasted_iota(jnp.int32, (128, 126), 1)
-    ).astype(BF16)
-
-    def turn_local(q, carry):
-        w = jnp.concatenate([lt[q], lt[q + 32]], axis=0)
-        mp[pl.ds(q, 128, stride=32), :] = dot_nt(eye, w)
-        return carry
-
-    lax.fori_loop(0, 32, turn_local, 0, unroll=4)
-
-    def unpack(source, target, n):
-        m = source[pl.ds(pl.multiple_of(n * 32, 32), 32), :].astype(BF16)
-        target[n] = jnp.concatenate([m[:, :64], m[:, 64:]], axis=0)
-
-    def unpack_local(g, carry):
-        for u in range(18):
-            unpack(mp, mb, g * 18 + u)
-        return carry
-
-    lax.fori_loop(0, 7, unpack_local, 0)
-
-    def lift(pair, weights):
-        return joined(dot_nn(split(pair), weights.reshape(128, 64)))
-
-    def level_pair(h, p):
-        return gath[col, p] if h == 0 else lev[lev_base(h) + p]
-
-    for h in range(HEIGHT - 1):
-        count = PAIRS >> h
-        off = level_offset(h)
-
-        def up_two(q, h=h, off=off):
-            one = lift(level_pair(h, 2 * q), mb[pl.ds(off + 4 * q, 2)])
-            two = lift(level_pair(h, 2 * q + 1), mb[pl.ds(off + 4 * q + 2, 2)])
-            lev[lev_base(h + 1) + q] = jnp.concatenate([one, two], axis=1)
-
-        half = count // 2
-        group = min(half, 8)
-
-        def up_step(g, carry, up_two=up_two, group=group):
-            for u in range(group):
-                up_two(g * group + u)
-            return carry
-
-        lax.fori_loop(0, half // group, up_step, 0)
-    root = lift(lev[lev_base(5)], mb[pl.ds(level_offset(5), 2)])
-
-    def placed(value, parity):
-        return jnp.where(
-            (lane >= 64).astype(jnp.int32) == parity, jnp.concatenate([value, value], axis=1), 0.0
-        )
-
-    xr[col] = placed(root, core)
-    xr_copies = []
-    for i in range(1, COLS):
-        c = pltpu.make_async_remote_copy(
-            xr.at[col], xr.at[col], xr_s.at[i], xr_r.at[i],
-            device_id=(row, lax.rem(col + i, COLS)), device_id_type=MESH)
-        c.start()
-        xr_copies.append(c)
 
     def recv(owner, k, kind):
         pltpu.make_async_remote_copy(
@@ -263,6 +194,81 @@
         c.start()
         sends.append(c)
 
+    ut_c = load(ut_h, ut, 2)
+    us_c = load(us_h, us, 3)
+    lt_c.wait()
+    load_near(0)
+    ls_c = load(ls_h, ls, 4)
+    for k in range(1, NEAR_PARTS):
+        load_near(k)
+    bt_c = load(bt_h, bt, 5)
+    eye = (
+        lax.broadcasted_iota(jnp.int32, (128, 126), 0)
+        == lax.broadcasted_iota(jnp.int32, (128, 126), 1)
+    ).astype(BF16)
+
+    def turn_local(q, carry):
+        w = jnp.concatenate([lt[q], lt[q + 32]], axis=0)
+        mp[pl.ds(q, 128, stride=MAT), :] = dot_nt(eye, w)
+        return carry
+
+    lax.fori_loop(0, 32, turn_local, 0, unroll=4)
+
+    def unpack(source, target, n):
+        m = source[pl.ds(n * MAT, 32), :].astype(BF16)
+        target[n] = jnp.concatenate([m[:, :64], m[:, 64:]], axis=0)
+
+    def unpack_local(g, carry):
+        for u in range(18):
+            unpack(mp, mb, g * 18 + u)
+        return carry
+
+    lax.fori_loop(0, 7, unpack_local, 0)
+
+    relay_near(0)
+
+    def lift(pair, weights):
+        return joined(dot_nn(split(pair), weights.reshape(128, 64)))
+
+    def level_pair(h, p):
+        return gath[col, p] if h == 0 else lev[lev_base(h) + p]
+
+    for h in range(HEIGHT - 1):
+        count = PAIRS >> h
+        off = level_offset(h)
+
+        def up_two(q, h=h, off=off):
+            one = lift(level_pair(h, 2 * q), mb[pl.ds(off + 4 * q, 2)])
+            two = lift(level_pair(h, 2 * q + 1), mb[pl.ds(off + 4 * q + 2, 2)])
+            lev[lev_base(h + 1) + q] = jnp.concatenate([one, two], axis=1)
+
+        half = count // 2
+        group = min(half, 8)
+
+        def up_step(g, carry, up_two=up_two, group=group):
+            for u in range(group):
+                up_two(g * group + u)
+            return carry
+
+        lax.fori_loop(0, half // group, up_step, 0)
+    root = lift(lev[lev_base(5)], mb[pl.ds(level_offset(5), 2)])
+
+    def placed(value, parity):
+        return jnp.where(
+            (lane >= 64).astype(jnp.int32) == parity, jnp.concatenate([value, value], axis=1), 0.0
+        )
+
+    xr[col] = placed(root, core)
+    xr_copies = []
+    for i in range(1, COLS):
+        c = pltpu.make_async_remote_copy(
+            xr.at[col], xr.at[col], xr_s.at[i], xr_r.at[i],
+            device_id=(row, lax.rem(col + i, COLS)), device_id_type=MESH)
+        c.start()
+        xr_copies.append(c)
+
+    relay_near(1)
+
     ut_c.wait()
     us_c.wait()
     picks = lax.broadcasted_iota(jnp.int32, (64, 254), 0)
@@ -283,9 +289,9 @@
 
     def turn_upper(q, carry):
         w = jnp.concatenate([ut[q], ut[q + 32]], axis=0)
-        mu[pl.ds(q, 64, stride=32), :] = dot_nt(pick_u, w)
+        mu[pl.ds(q, 64, stride=MAT), :] = dot_nt(pick_u, w)
         w = jnp.concatenate([us[q], us[q + 32]], axis=0)
-        mp[pl.ds(q, 16, stride=32), :] = dot_nt(pick_s, w)
+        mp[pl.ds(q, 16, stride=MAT), :] = dot_nt(pick_s, w)
         return carry
 
     lax.fori_loop(0, 32, turn_upper, 0, unroll=4)
@@ -299,7 +305,7 @@
 
     lax.fori_loop(0, 4, unpack_upper, 0)
 
-    relay_near(0)
+    relay_near(2)
 
     for i in range(1, COLS):
         peer = lax.rem(col + COLS - i, COLS)
@@ -327,30 +333,44 @@
         c.start()
         zr_copies.append(c)
 
-    relay_near(1)
+    relay_near(3)
 
     halo_next.wait_recv()
     halo_prev.wait_recv()
     eh[0] = split(halo[0])
     eh[LEAVES + 1] = split(halo[1])
     leaf_first = device * LEAVES
+    zero = jnp.zeros((2 * RHS, LEAF), BF16)
 
     def near_part(k):
-        nb_c[k].wait()
+        pltpu.make_async_copy(
+            nb_h.at[pl.ds(k * per, per)], nb.at[pl.ds(k * per, per)], nb_sem.at[k]).wait()
+        pltpu.make_async_copy(
+            lc_h.at[pl.ds(k * lper, lper)], lc.at[pl.ds(k * lper, lper)], lc_sem.at[k]).wait()
 
         def near_step(g, carry):
-            for u in range(16):
-                s = k * per + g * 16 + u
-                source = jnp.clip(nsrc[s] - leaf_first + 1, 0, LEAVES + 1)
-                o = dot_nt(eh[source], nb[s])
-                prod[pl.ds(s, RHS, stride=SLOTS), :] = joined(o)
+            for u in range(12):
+                s = k * per + g * 24 + 2 * u
+                one, two = (
+                    eh[jnp.clip(nsrc[s + i] - leaf_first + 1, 0, LEAVES + 1)] for i in range(2))
+                lhs = jnp.concatenate(
+                    [jnp.concatenate([one, zero], axis=1), jnp.concatenate([zero, two], axis=1)],
+                    axis=0)
+                o = dot_nt(lhs, jnp.concatenate([nb[s], nb[s + 1]], axis=1))
+                prod[pl.ds(s, RHS, stride=SLOT_ROWS), :] = joined(o[:32])
+                prod[pl.ds(s + 1, RHS, stride=SLOT_ROWS), :] = joined(o[32:])
+                if u < 8:
+                    t = k * lper + g * 8 + u
+                    cp[t] = jnp.concatenate([lc[t, 0], lc[t, 1], lc[t, 2], lc[t, 3]], axis=1)
             return carry
 
-        lax.fori_loop(0, per // 16, near_step, 0)
+        lax.fori_loop(0, per // 24, near_step, 0)
 
     near_part(0)
+    relay_far(0)
+    relay_far(1)
     near_part(1)
-    relay_near(2)
+    relay_far(2)
     near_part(2)
 
     ls_c.wait()
@@ -373,7 +393,8 @@
 
         lax.fori_loop(0, count // group, sib_step, 0)
 
-    relay_near(3)
+    relay_far(3)
+    near_part(3)
 
     for i in range(1, ROWS):
         peer = lax.rem(row + ROWS - i, ROWS)
@@ -429,18 +450,6 @@
 
         lax.fori_loop(0, half // group, down_step, 0)
 
-    lc_c.wait()
-
-    def pack_leaf(g, carry):
-        for u in range(16):
-            t = g * 16 + u
-            cp[t] = jnp.concatenate([lc[t, 0], lc[t, 1], lc[t, 2], lc[t, 3]], axis=1)
-        return carry
-
-    lax.fori_loop(0, LEAVES // 16, pack_leaf, 0)
-
-    near_part(3)
-
     target = nt_v[...] - leaf_first
     slot = lax.broadcasted_iota(jnp.int32, (LEAVES, SLOTS), 1)
     one_hot = (
@@ -452,10 +461,10 @@
     def sum_step(g, carry):
         for u in range(4):
             r = g * 4 + u
-            x = prod[pl.ds(pl.multiple_of(r * SLOTS, SLOTS), SLOTS), :]
+            x = prod[pl.ds(r * SLOT_ROWS, SLOTS), :]
             high = x.astype(BF16)
             low = (x - high.astype(F32)).astype(BF16)
-            nacc[pl.ds(r, LEAVES, stride=RHS), :] = dot_nn(one_hot, high) + dot_nn(one_hot, low)
+            nacc[pl.ds(r, LEAVES, stride=LEAF_ROWS), :] = dot_nn(one_hot, high) + dot_nn(one_hot, low)
         return carry
 
     lax.fori_loop(0, RHS // 4, sum_step, 0)
@@ -473,8 +482,6 @@
 
         lax.fori_loop(0, PART // 8, dup_step, 0)
 
-    for k in range(CHUNKS):
-        relay_far(k)
     other = 1 - core
     for k in range(CHUNKS):
         dup_part(col, k)
@@ -495,23 +502,31 @@
     group_first = row * (LEAVES * COLS)
 
     def final_step(g, carry):
-        leaves = [g * FINAL + u for u in range(FINAL)]
-        lhs = []
-        for t in leaves:
+        pairs = [g * (FINAL // 2) + u for u in range(FINAL // 2)]
+
+        def listed_of(t):
             d = [dup[jnp.clip(lsrc[j, t] - group_first, 0, LEAVES * COLS - 1)]
                  for j in range(PARTNERS)]
-            lhs.append(jnp.concatenate(
-                [jnp.where(first_half2, d[0], d[1]), jnp.where(first_half2, d[2], d[3])], axis=1))
-        listed = [dot_nt(x, cp[t]) for x, t in zip(lhs, leaves)]
+            return jnp.concatenate(
+                [jnp.where(first_half2, d[0], d[1]), jnp.where(first_half2, d[2], d[3])], axis=1)
+
+        lhs = [jnp.concatenate([listed_of(2 * q), listed_of(2 * q + 1)], axis=0) for q in pairs]
+        listed = [dot_nt(x, cp[pl.ds(2 * q, 2)].reshape(128, 256)) for x, q in zip(lhs, pairs)]
         y0 = []
-        for u, o in enumerate(listed):
-            c = carried[g * (FINAL // 2) + u // 2]
-            y0.append(split(joined(o) + (c[:, :64] if u % 2 == 0 else c[:, 64:])))
-        starts = [pl.multiple_of(t * LEAF, LEAF) for t in leaves]
-        far = [dot_nn(y, bt[:, pl.ds(start, LEAF)]) for y, start in zip(y0, starts)]
-        for o, t, start in zip(far, leaves, starts):
-            near = nacc[pl.ds(pl.multiple_of(t * RHS, RHS), RHS), :]
-            out[:, pl.ds(start, LEAF)] = joined(o) + near
+        for o, q in zip(listed, pairs):
+            c = carried[q]
+            one = jnp.where(first_half, joined(o[:32]) + c, 0.0)
+            two = jnp.where(first_half, 0.0, joined(o[32:]) + c)
+            y0.append(jnp.concatenate([split(one), split(two)], axis=0))
+        starts = [pl.multiple_of(q * 2 * LEAF, 2 * LEAF) for q in pairs]
+        far = []
+        for y, start in zip(y0, starts):
+            w = bt[:, pl.ds(start, 2 * LEAF)]
+            far.append(dot_nn(y, jnp.concatenate([w[:, :LEAF], w[:, LEAF:]], axis=0)))
+        for o, q, start in zip(far, pairs, starts):
+            out[:, pl.ds(start, 2 * LEAF)] = jnp.concatenate(
+                [joined(o[:32]) + nacc[pl.ds(2 * q * LEAF_ROWS, RHS), :],
+                 joined(o[32:]) + nacc[pl.ds((2 * q + 1) * LEAF_ROWS, RHS), :]], axis=1)
         return carry
 
     lax.fori_loop(0, LEAVES // FINAL, final_step, 0)
@@ -547,9 +562,9 @@
             V((2, RHS, 128), F32),
             V((COLS, PAIRS, RHS, 128), F32),
             V((COLS * LEAVES, 32, 128), BF16),
-            V((128 * 32, 128), F32),
+            V((128 * MAT, 128), F32),
             V((126, 64, 64), BF16),
-            V((64 * 32, 128), F32),
+            V((64 * MAT, 128), F32),
             V((64, 64, 64), BF16),
             V((8, 64, 64), BF16),
             V((32, RHS, 128), F32),
@@ -559,11 +574,11 @@
             V((COLS, RHS, 128), F32),
             V((ROWS, RHS, 128), F32),
             V((22, RHS, 128), F32),
-            V((RHS * SLOTS, 128), F32),
-            V((LEAVES * RHS, 128), F32),
+            V((RHS * SLOT_ROWS, 128), F32),
+            V((LEAVES * LEAF_ROWS, 128), F32),
             V((LEAVES, 64, 256), BF16),
             V((RHS, 8192), F32),
-            dma((7,)), dma((NEAR_PARTS,)), dma((CHUNKS,)), dma, dma((2,)), dma((2,)),
+            dma((6,)), dma((NEAR_PARTS,)), dma((NEAR_PARTS,)), dma((CHUNKS,)), dma, dma((2,)), dma((2,)),
             dma((3, CHUNKS)), dma((4, CHUNKS)), dma((7, CHUNKS)),
             dma((COLS,)), dma((COLS,)), dma((ROWS,)), dma((ROWS,)),
         ],

time: 40.4 us -> 38.7 us (0.958)
  Pallas kernels: 37.7 us -> 36 us
    pallas_call x1, Pallas kernels: 37.7 us -> 36 us  [shards(): pl.pallas_call(kernel, out_shape=jax.ShapeDtypeStruct((RHS, LEAVES * LEAF...]
where the time goes in v3:
time: 38.7 us; the launch traced here: 38.5 us
  Pallas kernels  36 us (93%)
  local copies, waits for them, and re-layouts  1.87 us (5%)
  between operations  0.66 us (2%)
    pallas_call x1, Pallas kernels, shards(): pl.pallas_call(kernel, out_shape=jax.ShapeDtypeStruct((RHS, LEAVES * LEAF...  36 us
    unnamed x1, local copies, waits for them, and re-layouts  1.87 us

profile of v3, /device:TPU:1, one launch (start us, length us, event | category | flops | bytes accessed | tf_op | source)
XLA Modules:
  0.0 38.5 jit_solution(1139020882833991729)
XLA Ops:
  0.7 36.0 %h2_product.1 = f32[16,8192]{1,0:T(8,128)} custom-call(f32[16,8192]{1,0:T(8,128)} %em_h.1, bf16[64,8192]{1,0:T(8,128)(2,1)} %bs_h.1, bf16[64,8192]{1,0:T(8,128)(2,1)} %bt_h.1, bf16[64,64,126]{2,1,0:T(8,128)(2,1)} %bitcast.7, bf16[62,64,64]{2,1,0:T(8,128)(2,1)} %ls_h.1, bf16[64,64,254]{2,1,0:T(8,128)(2,1)} %bitcast.5, bf16[64,64,254]{2,1,0:T(8,128)(2,1)} %bitcast.6, ...), custom_call_target="tpu_custom_call" | custom-call | tf_op jit(solution)/shard_map/h2_product/pallas_call | solution.py:551
  36.6 1.9 %copy.16 = f32[16,8192]{1,0:T(8,128)} copy(f32[16,8192]{1,0:T(8,128)} %h2_product.1) | data formatting | bytes 1048576

commit v4 on v3

--- a/solution.py
+++ b/solution.py
@@ -19,7 +19,7 @@
 PARTNERS = 4
 SLOTS = 192
 ROWS, COLS = 16, 8
-CHUNKS = 4
+CHUNKS = 2
 PART = PAIRS // CHUNKS
 HEIGHT = 6
 NEAR_PARTS = 4
@@ -56,11 +56,11 @@
 
 def kernel(
     em_h, bs_h, bt_h, lt_h, ls_h, ut_h, us_h, lsrc, lc_h, nb_h, nt_v, nsrc, ncnt,
-    out_h,
+    out,
     em, bs, bt, lt, ls, ut, us, lc, nb,
     eh, halo, gath, dup, mp, mb, mu, eu, su, lev, sib, ylev, carried,
-    xr, zr, upair, prod, nacc, cp, out,
-    load_sem, nb_sem, lc_sem, bs_sem, out_sem, halo_s, halo_r,
+    xr, zr, upair, prod, nacc, cp,
+    load_sem, nb_sem, lc_sem, bs_sem, halo_s, halo_r,
     own_s, fwd_s, gath_r, xr_s, xr_r, zr_s, zr_r,
 ):
     row, col = lax.axis_index("row"), lax.axis_index("col")
@@ -122,17 +122,6 @@
 
     lax.fori_loop(0, LEAVES // 8, split_leaf, 0)
 
-    pl.semaphore_wait(barrier, COLS - 1 + ROWS - 1 + 2)
-
-    halo_next = pltpu.make_async_remote_copy(
-        em.at[:, pl.ds((LEAVES - 1) * LEAF, LEAF)], halo.at[0], halo_s.at[0], halo_r.at[0],
-        device_id=next_id, device_id_type=MESH)
-    halo_prev = pltpu.make_async_remote_copy(
-        em.at[:, pl.ds(0, LEAF)], halo.at[1], halo_s.at[1], halo_r.at[1],
-        device_id=prev_id, device_id_type=MESH)
-    halo_next.start()
-    halo_prev.start()
-
     def piece(owner, k):
         return gath.at[owner, pl.ds(k * PART, PART)]
 
@@ -142,6 +131,11 @@
             device_id=(row, to_col), device_id_type=MESH)
 
     sends = []
+
+    def begin(owner, k, to_col, send_sem, kind):
+        c = send(owner, k, to_col, send_sem, kind)
+        c.start()
+        sends.append(c)
 
     def leaf_pair(p):
         a = eh[pl.ds(2 * p + 1, 2)].reshape(64, 128)
@@ -160,39 +154,30 @@
             return carry
 
         lax.fori_loop(0, PART // 8, leaf_step, 0)
-        for n, (to_col, kind) in enumerate(((up_col, 1), (down_col, 2), (sibling, 0))):
-            c = send(col, k, to_col, own_s.at[n, k], kind)
-            c.start()
-            sends.append(c)
 
     def recv(owner, k, kind):
         pltpu.make_async_remote_copy(
             piece(owner, k), piece(owner, k), own_s.at[0, k], gath_r.at[kind, k],
             device_id=(row, col), device_id_type=MESH).wait_recv()
 
-    def relay_near(k):
-        recv(down_col, k, 1)
-        if k < CHUNKS // 2:
-            c = send(down_col, k, up_col, fwd_s.at[0, k], 3)
-            c.start()
-            sends.append(c)
-        c = send(down_col, k, sibling, fwd_s.at[1, k], 4)
-        c.start()
-        sends.append(c)
-        recv(up_col, k, 2)
-        if k >= CHUNKS // 2:
-            c = send(up_col, k, down_col, fwd_s.at[0, k], 3)
-            c.start()
-            sends.append(c)
-        c = send(up_col, k, sibling, fwd_s.at[2, k], 5)
-        c.start()
-        sends.append(c)
-
-    def relay_far(k):
-        recv(far_col, k, 3)
-        c = send(far_col, k, sibling, fwd_s.at[3, k], 6)
-        c.start()
-        sends.append(c)
+    def relay_first():
+        recv(down_col, 0, 1)
+        begin(down_col, 0, up_col, fwd_s.at[0, 0], 3)
+        recv(up_col, 1, 2)
+        begin(up_col, 1, down_col, fwd_s.at[0, 1], 3)
+        begin(down_col, 0, sibling, fwd_s.at[1, 0], 4)
+        begin(up_col, 1, sibling, fwd_s.at[2, 1], 5)
+
+    def relay_second():
+        recv(down_col, 1, 1)
+        begin(down_col, 1, sibling, fwd_s.at[1, 1], 4)
+        recv(up_col, 0, 2)
+        begin(up_col, 0, sibling, fwd_s.at[2, 0], 5)
+
+    def relay_far():
+        for k in range(CHUNKS):
+            recv(far_col, k, 3)
+            begin(far_col, k, sibling, fwd_s.at[3, k], 6)
 
     ut_c = load(ut_h, ut, 2)
     us_c = load(us_h, us, 3)
@@ -225,10 +210,17 @@
 
     lax.fori_loop(0, 7, unpack_local, 0)
 
-    relay_near(0)
-
     def lift(pair, weights):
         return joined(dot_nn(split(pair), weights.reshape(128, 64)))
+
+    zero = jnp.zeros((2 * RHS, LEAF), BF16)
+
+    def lift_two(one, two, weights):
+        lhs = jnp.concatenate(
+            [jnp.concatenate([split(one), zero], axis=1),
+             jnp.concatenate([zero, split(two)], axis=1)], axis=0)
+        o = dot_nn(lhs, weights.reshape(256, 64))
+        return jnp.concatenate([joined(o[:32]), joined(o[32:])], axis=1)
 
     def level_pair(h, p):
         return gath[col, p] if h == 0 else lev[lev_base(h) + p]
@@ -238,9 +230,8 @@
         off = level_offset(h)
 
         def up_two(q, h=h, off=off):
-            one = lift(level_pair(h, 2 * q), mb[pl.ds(off + 4 * q, 2)])
-            two = lift(level_pair(h, 2 * q + 1), mb[pl.ds(off + 4 * q + 2, 2)])
-            lev[lev_base(h + 1) + q] = jnp.concatenate([one, two], axis=1)
+            lev[lev_base(h + 1) + q] = lift_two(
+                level_pair(h, 2 * q), level_pair(h, 2 * q + 1), mb[pl.ds(off + 4 * q, 4)])
 
         half = count // 2
         group = min(half, 8)
@@ -259,6 +250,17 @@
         )
 
     xr[col] = placed(root, core)
+    pl.semaphore_wait(barrier, COLS - 1 + ROWS - 1 + 2)
+
+    halo_next = pltpu.make_async_remote_copy(
+        em.at[:, pl.ds((LEAVES - 1) * LEAF, LEAF)], halo.at[0], halo_s.at[0], halo_r.at[0],
+        device_id=next_id, device_id_type=MESH)
+    halo_prev = pltpu.make_async_remote_copy(
+        em.at[:, pl.ds(0, LEAF)], halo.at[1], halo_s.at[1], halo_r.at[1],
+        device_id=prev_id, device_id_type=MESH)
+    halo_next.start()
+    halo_prev.start()
+
     xr_copies = []
     for i in range(1, COLS):
         c = pltpu.make_async_remote_copy(
@@ -267,7 +269,12 @@
         c.start()
         xr_copies.append(c)
 
-    relay_near(1)
+    begin(col, 0, up_col, own_s.at[0, 0], 1)
+    begin(col, 1, down_col, own_s.at[1, 1], 2)
+    for k in range(CHUNKS):
+        begin(col, k, sibling, own_s.at[2, k], 0)
+    begin(col, 1, up_col, own_s.at[0, 1], 1)
+    begin(col, 0, down_col, own_s.at[1, 0], 2)
 
     ut_c.wait()
     us_c.wait()
@@ -305,43 +312,11 @@
 
     lax.fori_loop(0, 4, unpack_upper, 0)
 
-    relay_near(2)
-
-    for i in range(1, COLS):
-        peer = lax.rem(col + COLS - i, COLS)
-        pltpu.make_async_remote_copy(
-            xr.at[peer], xr.at[peer], xr_s.at[i], xr_r.at[i],
-            device_id=(row, peer), device_id_type=MESH).wait_recv()
-    for i in range(4):
-        upair[i] = xr[2 * i] + xr[2 * i + 1]
-
-    def up_upper(source, count, target, first):
-        for i in range(count // 2):
-            one = lift(upair[source + 2 * i], eu[first + 4 * i : first + 4 * i + 2])
-            two = lift(upair[source + 2 * i + 1], eu[first + 4 * i + 2 : first + 4 * i + 4])
-            upair[target + i] = jnp.concatenate([one, two], axis=1)
-
-    up_upper(0, 4, 4, 0)
-    up_upper(4, 2, 6, 8)
-    row_root = lift(upair[6], eu[12:14])
-    zr[row] = placed(row_root, lax.rem(row, 2))
-    zr_copies = []
-    for i in range(1, ROWS):
-        c = pltpu.make_async_remote_copy(
-            zr.at[row], zr.at[row], zr_s.at[i], zr_r.at[i],
-            device_id=(lax.rem(row + i, ROWS), col), device_id_type=MESH)
-        c.start()
-        zr_copies.append(c)
-
-    relay_near(3)
-
     halo_next.wait_recv()
     halo_prev.wait_recv()
     eh[0] = split(halo[0])
     eh[LEAVES + 1] = split(halo[1])
     leaf_first = device * LEAVES
-    zero = jnp.zeros((2 * RHS, LEAF), BF16)
-
     def near_part(k):
         pltpu.make_async_copy(
             nb_h.at[pl.ds(k * per, per)], nb.at[pl.ds(k * per, per)], nb_sem.at[k]).wait()
@@ -367,11 +342,37 @@
         lax.fori_loop(0, per // 24, near_step, 0)
 
     near_part(0)
-    relay_far(0)
-    relay_far(1)
+
+    for i in range(1, COLS):
+        peer = lax.rem(col + COLS - i, COLS)
+        pltpu.make_async_remote_copy(
+            xr.at[peer], xr.at[peer], xr_s.at[i], xr_r.at[i],
+            device_id=(row, peer), device_id_type=MESH).wait_recv()
+    for i in range(4):
+        upair[i] = xr[2 * i] + xr[2 * i + 1]
+
+    def up_upper(source, count, target, first):
+        for i in range(count // 2):
+            upair[target + i] = lift_two(
+                upair[source + 2 * i], upair[source + 2 * i + 1],
+                eu[first + 4 * i : first + 4 * i + 4])
+
+    up_upper(0, 4, 4, 0)
+    up_upper(4, 2, 6, 8)
+    row_root = lift(upair[6], eu[12:14])
+    zr[row] = placed(row_root, lax.rem(row, 2))
+    zr_copies = []
+    for i in range(1, ROWS):
+        c = pltpu.make_async_remote_copy(
+            zr.at[row], zr.at[row], zr_s.at[i], zr_r.at[i],
+            device_id=(lax.rem(row + i, ROWS), col), device_id_type=MESH)
+        c.start()
+        zr_copies.append(c)
+
     near_part(1)
-    relay_far(2)
     near_part(2)
+    relay_first()
+    near_part(3)
 
     ls_c.wait()
     for h in range(1, HEIGHT):
@@ -393,8 +394,47 @@
 
         lax.fori_loop(0, count // group, sib_step, 0)
 
-    relay_far(3)
-    near_part(3)
+    target = nt_v[...] - leaf_first
+    slot = lax.broadcasted_iota(jnp.int32, (LEAVES, SLOTS), 1)
+    one_hot = (
+        (jnp.broadcast_to(target, (LEAVES, SLOTS))
+         == lax.broadcasted_iota(jnp.int32, (LEAVES, SLOTS), 0))
+        & (slot < ncnt[0])
+    ).astype(BF16)
+
+    def sum_step(g, carry):
+        for u in range(4):
+            r = g * 4 + u
+            x = prod[pl.ds(r * SLOT_ROWS, SLOTS), :]
+            high = x.astype(BF16)
+            low = (x - high.astype(F32)).astype(BF16)
+            nacc[pl.ds(r, LEAVES, stride=LEAF_ROWS), :] = dot_nn(one_hot, high) + dot_nn(one_hot, low)
+        return carry
+
+    lax.fori_loop(0, RHS // 4, sum_step, 0)
+
+    relay_second()
+
+    def dup_part(owner, k):
+        def dup_step(g, carry):
+            for u in range(8):
+                p = k * PART + g * 8 + u
+                x = gath[owner, p]
+                turned = jnp.concatenate([x[:, 64:], x[:, :64]], axis=1)
+                base = owner * LEAVES + 2 * p
+                dup[base] = split(jnp.where(first_half, x, turned))
+                dup[base + 1] = split(jnp.where(first_half, turned, x))
+            return carry
+
+        lax.fori_loop(0, PART // 8, dup_step, 0)
+
+    twin = 1 - core
+    for k in range(CHUNKS):
+        dup_part(col, k)
+        dup_part(down_col, k)
+        dup_part(up_col, k)
+        recv(sibling, k, 0)
+        dup_part(sibling, k)
 
     for i in range(1, ROWS):
         peer = lax.rem(row + ROWS - i, ROWS)
@@ -418,6 +458,8 @@
         other = jnp.where(lax.rem(mine, 2) == 1, pair, turned)[:, :64]
         y = joined(dot_nt(split(other), su[j])) + joined(dot_nt(split(y), eu[48 + j]))
 
+    relay_far()
+
     ylev[30] = placed(y, 0)
     for h in range(HEIGHT - 1, -1, -1):
         count = PAIRS >> h
@@ -450,53 +492,16 @@
 
         lax.fori_loop(0, half // group, down_step, 0)
 
-    target = nt_v[...] - leaf_first
-    slot = lax.broadcasted_iota(jnp.int32, (LEAVES, SLOTS), 1)
-    one_hot = (
-        (jnp.broadcast_to(target, (LEAVES, SLOTS))
-         == lax.broadcasted_iota(jnp.int32, (LEAVES, SLOTS), 0))
-        & (slot < ncnt[0])
-    ).astype(BF16)
-
-    def sum_step(g, carry):
-        for u in range(4):
-            r = g * 4 + u
-            x = prod[pl.ds(r * SLOT_ROWS, SLOTS), :]
-            high = x.astype(BF16)
-            low = (x - high.astype(F32)).astype(BF16)
-            nacc[pl.ds(r, LEAVES, stride=LEAF_ROWS), :] = dot_nn(one_hot, high) + dot_nn(one_hot, low)
-        return carry
-
-    lax.fori_loop(0, RHS // 4, sum_step, 0)
-
-    def dup_part(owner, k):
-        def dup_step(g, carry):
-            for u in range(8):
-                p = k * PART + g * 8 + u
-                x = gath[owner, p]
-                turned = jnp.concatenate([x[:, 64:], x[:, :64]], axis=1)
-                base = owner * LEAVES + 2 * p
-                dup[base] = split(jnp.where(first_half, x, turned))
-                dup[base + 1] = split(jnp.where(first_half, turned, x))
-            return carry
-
-        lax.fori_loop(0, PART // 8, dup_step, 0)
-
-    other = 1 - core
     for k in range(CHUNKS):
-        dup_part(col, k)
-        dup_part(down_col, k)
-        dup_part(up_col, k)
-        recv(sibling, k, 0)
-        dup_part(sibling, k)
-        recv(zprev * 2 + other, k, 4)
-        dup_part(zprev * 2 + other, k)
-        recv(znext * 2 + other, k, 5)
-        dup_part(znext * 2 + other, k)
+        recv(zprev * 2 + twin, k, 4)
+        dup_part(zprev * 2 + twin, k)
+        recv(znext * 2 + twin, k, 5)
+        dup_part(znext * 2 + twin, k)
     for k in range(CHUNKS):
         dup_part(far_col, k)
-        recv(zfar * 2 + other, k, 6)
-        dup_part(zfar * 2 + other, k)
+    for k in range(CHUNKS):
+        recv(zfar * 2 + twin, k, 6)
+        dup_part(zfar * 2 + twin, k)
 
     bt_c.wait()
     group_first = row * (LEAVES * COLS)
@@ -530,13 +535,10 @@
         return carry
 
     lax.fori_loop(0, LEAVES // FINAL, final_step, 0)
-    out_c = pltpu.make_async_copy(out, out_h, out_sem)
-    out_c.start()
     halo_next.wait_send()
     halo_prev.wait_send()
     for c in sends + xr_copies + zr_copies:
         c.wait_send()
-    out_c.wait()
 
 
 def shards(
@@ -550,9 +552,9 @@
     V = pltpu.VMEM
     return pl.pallas_call(
         kernel,
-        out_shape=jax.ShapeDtypeStruct((RHS, LEAVES * LEAF), F32),
+        out_shape=V((RHS, LEAVES * LEAF), F32),
         in_specs=[hbm] * 7 + [smem, hbm, hbm, vmem, smem, smem],
-        out_specs=hbm,
+        out_specs=vmem,
         scratch_shapes=[
             V((RHS, 8192), F32), V((RANK, 8192), BF16), V((RANK, 8192), BF16),
             V((64, 64, 126), BF16), V((62, 64, 64), BF16),
@@ -577,8 +579,7 @@
             V((RHS * SLOT_ROWS, 128), F32),
             V((LEAVES * LEAF_ROWS, 128), F32),
             V((LEAVES, 64, 256), BF16),
-            V((RHS, 8192), F32),
-            dma((6,)), dma((NEAR_PARTS,)), dma((NEAR_PARTS,)), dma((CHUNKS,)), dma, dma((2,)), dma((2,)),
+            dma((6,)), dma((NEAR_PARTS,)), dma((NEAR_PARTS,)), dma((CHUNKS,)), dma((2,)), dma((2,)),
             dma((3, CHUNKS)), dma((4, CHUNKS)), dma((7, CHUNKS)),
             dma((COLS,)), dma((COLS,)), dma((ROWS,)), dma((ROWS,)),
         ],

time: 38.7 us -> 33.9 us (0.88)
  the two profiles are of different devices: /device:TPU:1 before, /device:TPU:0 now
where the time goes in v4:
time: 33.9 us; the launch traced here: 33.8 us
  Pallas kernels  32.3 us (95%)
  local copies, waits for them, and re-layouts  0.8 us (2%)
  between operations  0.66 us (2%)
    pallas_call x1, Pallas kernels, shards(): pl.pallas_call(kernel, out_shape=V((RHS, LEAVES * LEAF), F32), in_specs=[...  32.3 us
    unnamed x1, local copies, waits for them, and re-layouts  0.8 us

profile of v4, /device:TPU:0, one launch (start us, length us, event | category | flops | bytes accessed | tf_op | source)
XLA Modules:
  0.0 33.8 jit_solution(972913283781346583)
XLA Ops:
  0.7 32.3 %h2_product.1 = f32[16,8192]{1,0:T(8,128)S(1)} custom-call(f32[16,8192]{1,0:T(8,128)} %em_h.1, bf16[64,8192]{1,0:T(8,128)(2,1)} %bs_h.1, bf16[64,8192]{1,0:T(8,128)(2,1)} %bt_h.1, bf16[64,64,126]{2,1,0:T(8,128)(2,1)} %bitcast.7, bf16[62,64,64]{2,1,0:T(8,128)(2,1)} %ls_h.1, bf16[64,64,254]{2,1,0:T(8,128)(2,1)} %bitcast.5, bf16[64,64,254]{2,1,0:T(8,128)(2,1)} %bitcast.6, ...), custom_call_target="tpu_custom_call" | custom-call | tf_op jit(solution)/shard_map/h2_product/pallas_call | solution.py:553
  33.0 0.8 %copy.15 = f32[16,8192]{1,0:T(8,128)} copy(f32[16,8192]{1,0:T(8,128)S(1)} %h2_product.1) | data formatting | bytes 1048576

commit v5 on v4

--- a/solution.py
+++ b/solution.py
@@ -317,6 +317,14 @@
     eh[0] = split(halo[0])
     eh[LEAVES + 1] = split(halo[1])
     leaf_first = device * LEAVES
+    def sib_one(i):
+        x = lev[i]
+        lhs = jnp.concatenate([split(x[:, 64:]), split(x[:, :64])], axis=0)
+        o = dot_nt(lhs, ls[pl.ds(2 * i, 2)].reshape(128, 64))
+        sib[i] = jnp.where(first_half, o[0:16] + o[16:32], o[32:48] + o[48:64])
+
+    ls_c.wait()
+
     def near_part(k):
         pltpu.make_async_copy(
             nb_h.at[pl.ds(k * per, per)], nb.at[pl.ds(k * per, per)], nb_sem.at[k]).wait()
@@ -334,6 +342,8 @@
                 o = dot_nt(lhs, jnp.concatenate([nb[s], nb[s + 1]], axis=1))
                 prod[pl.ds(s, RHS, stride=SLOT_ROWS), :] = joined(o[:32])
                 prod[pl.ds(s + 1, RHS, stride=SLOT_ROWS), :] = joined(o[32:])
+                if u < 4:
+                    sib_one(lax.rem((2 * k + g) * 4 + u, PAIRS - 1))
                 if u < 8:
                     t = k * lper + g * 8 + u
                     cp[t] = jnp.concatenate([lc[t, 0], lc[t, 1], lc[t, 2], lc[t, 3]], axis=1)
@@ -374,26 +384,6 @@
     relay_first()
     near_part(3)
 
-    ls_c.wait()
-    for h in range(1, HEIGHT):
-        count = PAIRS >> h
-
-        def sib_one(p, h=h):
-            x = lev[lev_base(h) + p]
-            lhs = jnp.concatenate([split(x[:, 64:]), split(x[:, :64])], axis=0)
-            w = ls[pl.ds(LEAVES - 2 * (LEAVES >> h) + 2 * p, 2)].reshape(128, 64)
-            o = dot_nt(lhs, w)
-            sib[lev_base(h) + p] = jnp.where(first_half, o[0:16] + o[16:32], o[32:48] + o[48:64])
-
-        group = min(count, 8)
-
-        def sib_step(g, carry, sib_one=sib_one, group=group):
-            for u in range(group):
-                sib_one(g * group + u)
-            return carry
-
-        lax.fori_loop(0, count // group, sib_step, 0)
-
     target = nt_v[...] - leaf_first
     slot = lax.broadcasted_iota(jnp.int32, (LEAVES, SLOTS), 1)
     one_hot = (
@@ -402,39 +392,47 @@
         & (slot < ncnt[0])
     ).astype(BF16)
 
-    def sum_step(g, carry):
-        for u in range(4):
-            r = g * 4 + u
-            x = prod[pl.ds(r * SLOT_ROWS, SLOTS), :]
-            high = x.astype(BF16)
-            low = (x - high.astype(F32)).astype(BF16)
-            nacc[pl.ds(r, LEAVES, stride=LEAF_ROWS), :] = dot_nn(one_hot, high) + dot_nn(one_hot, low)
-        return carry
-
-    lax.fori_loop(0, RHS // 4, sum_step, 0)
-
     relay_second()
 
-    def dup_part(owner, k):
+    def dup_pair(owner, p):
+        x = gath[owner, p]
+        turned = jnp.concatenate([x[:, 64:], x[:, :64]], axis=1)
+        base = owner * LEAVES + 2 * p
+        dup[base] = split(jnp.where(first_half, x, turned))
+        dup[base + 1] = split(jnp.where(first_half, turned, x))
+
+    def dup_all(owner):
         def dup_step(g, carry):
-            for u in range(8):
-                p = k * PART + g * 8 + u
-                x = gath[owner, p]
-                turned = jnp.concatenate([x[:, 64:], x[:, :64]], axis=1)
-                base = owner * LEAVES + 2 * p
-                dup[base] = split(jnp.where(first_half, x, turned))
-                dup[base + 1] = split(jnp.where(first_half, turned, x))
+            for u in range(16):
+                dup_pair(owner, g * 16 + u)
             return carry
 
-        lax.fori_loop(0, PART // 8, dup_step, 0)
+        lax.fori_loop(0, PAIRS // 16, dup_step, 0)
 
     twin = 1 - core
     for k in range(CHUNKS):
-        dup_part(col, k)
-        dup_part(down_col, k)
-        dup_part(up_col, k)
         recv(sibling, k, 0)
-        dup_part(sibling, k)
+    for first, owner in ((0, col), (4, down_col), (8, up_col), (12, sibling)):
+
+        def sum_step(g, carry, first=first, owner=owner):
+            for u in range(2):
+                r = first + g * 2 + u
+                x = prod[pl.ds(r * SLOT_ROWS, SLOTS), :]
+                high = x.astype(BF16)
+                low = (x - high.astype(F32)).astype(BF16)
+                nacc[pl.ds(r, LEAVES, stride=LEAF_ROWS), :] = (
+                    dot_nn(one_hot, high) + dot_nn(one_hot, low))
+                for v in range(8):
+                    dup_pair(owner, g * 16 + u * 8 + v)
+            return carry
+
+        lax.fori_loop(0, 2, sum_step, 0)
+    for kind, owner in ((4, zprev * 2 + twin), (5, znext * 2 + twin)):
+        for k in range(CHUNKS):
+            recv(owner, k, kind)
+        dup_all(owner)
+    relay_far()
+    dup_all(far_col)
 
     for i in range(1, ROWS):
         peer = lax.rem(row + ROWS - i, ROWS)
@@ -458,8 +456,6 @@
         other = jnp.where(lax.rem(mine, 2) == 1, pair, turned)[:, :64]
         y = joined(dot_nt(split(other), su[j])) + joined(dot_nt(split(y), eu[48 + j]))
 
-    relay_far()
-
     ylev[30] = placed(y, 0)
     for h in range(HEIGHT - 1, -1, -1):
         count = PAIRS >> h
@@ -493,15 +489,8 @@
         lax.fori_loop(0, half // group, down_step, 0)
 
     for k in range(CHUNKS):
-        recv(zprev * 2 + twin, k, 4)
-        dup_part(zprev * 2 + twin, k)
-        recv(znext * 2 + twin, k, 5)
-        dup_part(znext * 2 + twin, k)
-    for k in range(CHUNKS):
-        dup_part(far_col, k)
-    for k in range(CHUNKS):
         recv(zfar * 2 + twin, k, 6)
-        dup_part(zfar * 2 + twin, k)
+    dup_all(zfar * 2 + twin)
 
     bt_c.wait()
     group_first = row * (LEAVES * COLS)

time: 33.9 us -> 32.9 us (0.971)
  the two profiles are of different devices: /device:TPU:0 before, /device:TPU:1 now
where the time goes in v5:
time: 32.9 us; the launch traced here: 32.7 us
  Pallas kernels  31.3 us (95%)
  local copies, waits for them, and re-layouts  0.8 us (2%)
  between operations  0.66 us (2%)
    pallas_call x1, Pallas kernels, shards(): pl.pallas_call(kernel, out_shape=V((RHS, LEAVES * LEAF), F32), in_specs=[...  31.3 us
    unnamed x1, local copies, waits for them, and re-layouts  0.8 us

profile of v5, /device:TPU:1, one launch (start us, length us, event | category | flops | bytes accessed | tf_op | source)
XLA Modules:
  0.0 32.7 jit_solution(13815142683865826296)
XLA Ops:
  0.7 31.3 %h2_product.1 = f32[16,8192]{1,0:T(8,128)S(1)} custom-call(f32[16,8192]{1,0:T(8,128)} %em_h.1, bf16[64,8192]{1,0:T(8,128)(2,1)} %bs_h.1, bf16[64,8192]{1,0:T(8,128)(2,1)} %bt_h.1, bf16[64,64,126]{2,1,0:T(8,128)(2,1)} %bitcast.7, bf16[62,64,64]{2,1,0:T(8,128)(2,1)} %ls_h.1, bf16[64,64,254]{2,1,0:T(8,128)(2,1)} %bitcast.5, bf16[64,64,254]{2,1,0:T(8,128)(2,1)} %bitcast.6, ...), custom_call_target="tpu_custom_call" | custom-call | tf_op jit(solution)/shard_map/h2_product/pallas_call | solution.py:542
  31.9 0.8 %copy.15 = f32[16,8192]{1,0:T(8,128)} copy(f32[16,8192]{1,0:T(8,128)S(1)} %h2_product.1) | data formatting | bytes 1048576

commit v6 on v5

--- a/solution.py
+++ b/solution.py
@@ -258,8 +258,6 @@
     halo_prev = pltpu.make_async_remote_copy(
         em.at[:, pl.ds(0, LEAF)], halo.at[1], halo_s.at[1], halo_r.at[1],
         device_id=prev_id, device_id_type=MESH)
-    halo_next.start()
-    halo_prev.start()
 
     xr_copies = []
     for i in range(1, COLS):
@@ -269,6 +267,8 @@
         c.start()
         xr_copies.append(c)
 
+    halo_next.start()
+    halo_prev.start()
     begin(col, 0, up_col, own_s.at[0, 0], 1)
     begin(col, 1, down_col, own_s.at[1, 1], 2)
     for k in range(CHUNKS):
@@ -433,6 +433,11 @@
         dup_all(owner)
     relay_far()
     dup_all(far_col)
+
+    halo_next.wait_send()
+    halo_prev.wait_send()
+    for c in sends[:-CHUNKS] + xr_copies + zr_copies:
+        c.wait_send()
 
     for i in range(1, ROWS):
         peer = lax.rem(row + ROWS - i, ROWS)
@@ -524,9 +529,7 @@
         return carry
 
     lax.fori_loop(0, LEAVES // FINAL, final_step, 0)
-    halo_next.wait_send()
-    halo_prev.wait_send()
-    for c in sends + xr_copies + zr_copies:
+    for c in sends[-CHUNKS:]:
         c.wait_send()
 
 

time: 32.9 us -> 32.9 us (level)
  no operation moved by 1% of the time
where the time goes in v6:
time: 32.9 us; the launch traced here: 32.7 us
  Pallas kernels  31.3 us (95%)
  local copies, waits for them, and re-layouts  0.8 us (2%)
  between operations  0.66 us (2%)
    pallas_call x1, Pallas kernels, shards(): pl.pallas_call(kernel, out_shape=V((RHS, LEAVES * LEAF), F32), in_specs=[...  31.3 us
    unnamed x1, local copies, waits for them, and re-layouts  0.8 us

profile of v6, /device:TPU:1, one launch (start us, length us, event | category | flops | bytes accessed | tf_op | source)
XLA Modules:
  0.0 32.7 jit_solution(8496671134093453447)
XLA Ops:
  0.7 31.3 %h2_product.1 = f32[16,8192]{1,0:T(8,128)S(1)} custom-call(f32[16,8192]{1,0:T(8,128)} %em_h.1, bf16[64,8192]{1,0:T(8,128)(2,1)} %bs_h.1, bf16[64,8192]{1,0:T(8,128)(2,1)} %bt_h.1, bf16[64,64,126]{2,1,0:T(8,128)(2,1)} %bitcast.7, bf16[62,64,64]{2,1,0:T(8,128)(2,1)} %ls_h.1, bf16[64,64,254]{2,1,0:T(8,128)(2,1)} %bitcast.5, bf16[64,64,254]{2,1,0:T(8,128)(2,1)} %bitcast.6, ...), custom_call_target="tpu_custom_call" | custom-call | tf_op jit(solution)/shard_map/h2_product/pallas_call | solution.py:545
  31.9 0.8 %copy.15 = f32[16,8192]{1,0:T(8,128)} copy(f32[16,8192]{1,0:T(8,128)S(1)} %h2_product.1) | data formatting | bytes 1048576
